TPU v7x, 128 devices: a whole 4x4x4 slice. The times are simulated.
128 devices in a mesh: dp: 2 (over core), tensor: 64 (over z, y, x).
Axes of the slice: x: 4, y: 4, z: 4, core: 2. Of those that a mesh axis runs over, the one named last changes fastest.
Arguments:
- activations: bfloat16 [4096, 5120], P(('dp', 'tensor')), may hold values from -7 to 7
- head_grads: bfloat16 [4096, 2048], P('dp', 'tensor'), may hold values from -10 to 10
- momentum: bfloat16 [2, 64, 80, 2048], P('dp', 'tensor'), may hold values from -6 to 6
Outputs:
- new_momentum: bfloat16 [2, 64, 80, 2048], P('dp', 'tensor')
- update: bfloat16 [64, 80, 2048], P('tensor')
All inputs are finite; a program needn't handle non-finite values.
Results may differ from a plain program's by a relative error of at most 0.001.
Values may be sent and summed in bfloat16 or wider, within the bound.
A program may use at most 128 MiB of HBM per device.

v0:
```python
import math

import jax
import jax.numpy as jnp
from jax import lax
from jax.sharding import PartitionSpec as P

BLOCK = 64
KEEP = 8


def dct_basis():
    frequency = jnp.arange(KEEP, dtype=jnp.float32)[:, None]
    position = jnp.arange(BLOCK, dtype=jnp.float32)[None, :]
    normalizer = jnp.where(frequency == 0, math.sqrt(1.0 / BLOCK), math.sqrt(2.0 / BLOCK))
    return normalizer * jnp.cos(math.pi * (2.0 * position + 1.0) * frequency / (2.0 * BLOCK))


def forward_part(values, basis_table, part_table):
    rows_here, rblocks, col_count = values.shape
    blocks = values.reshape(rows_here, rblocks, col_count // BLOCK, BLOCK)
    spectrum = jnp.einsum(
        "kn,nabm,lm->klab", part_table, blocks, basis_table, precision=lax.Precision.HIGHEST
    )
    return spectrum.reshape(KEEP, KEEP, rblocks * (col_count // BLOCK))


def kept_part(spectrum, basis_table, part_table, rblocks):
    cblocks = spectrum.shape[2] // rblocks
    shaped = spectrum.reshape(KEEP, KEEP, rblocks, cblocks)
    values = jnp.einsum(
        "kn,klab,lm->nabm", part_table, shaped, basis_table, precision=lax.Precision.HIGHEST
    )
    return values.reshape(part_table.shape[1], rblocks, cblocks * BLOCK)


def body(activations, head_grads, momentum):
    basis_table = dct_basis()
    local_tokens, model_width = activations.shape
    rblocks = model_width // BLOCK
    local_cols = head_grads.shape[1]
    splits = lax.axis_size("tensor")
    rows_here = BLOCK // splits
    all_cols = local_cols * splits
    block_rows = lax.all_gather(activations, "tensor", axis=0, tiled=True)
    shaped = block_rows.reshape(block_rows.shape[0], rblocks, BLOCK)
    by_column = jnp.einsum("tan,tc->nac", shaped, head_grads, preferred_element_type=jnp.float32)
    gradient = lax.all_to_all(by_column, "tensor", split_axis=0, concat_axis=2, tiled=True)
    squares = lax.psum(jnp.sum(gradient * gradient), "tensor")
    root_mean = jnp.sqrt(squares / (model_width * all_cols) + 1e-06)
    factor = jnp.minimum(jnp.float32(1.0), 1.0 / root_mean)
    combined = 0.9 * momentum[0].astype(jnp.float32) + factor * gradient
    first_row = lax.axis_index("tensor") * rows_here
    part_table = lax.dynamic_slice_in_dim(basis_table, first_row, rows_here, 1)
    partial_value = forward_part(combined, basis_table, part_table)
    replicas = lax.axis_size("dp")
    spectrum = lax.psum(partial_value, "tensor")
    replica_total = lax.psum(spectrum, "dp")
    residual = combined - kept_part(spectrum, basis_table, part_table, rblocks)
    new_momentum = residual.astype(jnp.bfloat16)[None]
    averaged = replica_total / replicas
    update = kept_part(averaged, basis_table, part_table, rblocks).astype(jnp.bfloat16)
    return (new_momentum, update)


def solution(mesh):
    placed = (P(("dp", "tensor"), None), P("dp", "tensor"), P("dp", "tensor", None, None))
    return jax.shard_map(
        body,
        mesh=mesh,
        in_specs=placed,
        out_specs=(P("dp", "tensor", None, None), P("tensor", None, None)),
        check_vma=False,
    )
```

profile of v0, /device:TPU:1, one launch (start us, length us, event | category | flops | bytes accessed | tf_op | source)
XLA Modules:
  0.0 571.6 jit_solution(14034571070717383962)
XLA Ops:
  7.2 0.0 copy-start
  7.2 0.0 all-gather.2.cloned.1.call-start
  7.2 0.7 all-gather.2.cloned.1.call-update
  7.9 123.6 %all-gather.2.cloned.1.call-done = bf16[2048,5120]{1,0:T(8,128)(2,1)} async-done(((bf16[32,5120]{1,0:T(8,128)(2,1)}), bf16[2048,5120]{1,0:T(8,128)(2,1)}) %all-gather.2.cloned.1.call-update) | async-done | bytes 20971536 | tf_op jit(solution)/shard_map/all_gather | solution.py:45
  131.5 28.4 %copy.32 = bf16[2048,5120]{0,1:T(8,128)(2,1)} copy(bf16[2048,5120]{1,0:T(8,128)(2,1)} %all-gather.2.cloned.1.call-done) | data formatting | bytes 41943040 | tf_op jit(solution)/shard_map/all_gather | solution.py:45
  159.9 0.0 copy-done
  159.9 0.0 copy-start.1
  159.9 34.5 %fusion.2 = f32[64,80,32]{1,2,0:T(8,128)} fusion(bf16[2048,80,64]{0,2,1:T(8,128)(2,1)} %bitcast.39, bf16[2048,32]{0,1:T(8,128)(2,1)S(1)} %copy-done), kind=kOutput, calls=%fused_computation.2 | convolution fusion | flops 671088640 | bytes 21757952 | tf_op jit(solution)/shard_map/tan,tc->nac/dot_general | solution.py:47
  194.4 8.4 %all-to-all-start = ((f32[64,80,32]{1,2,0:T(8,128)}), f32[64,80,32]{1,2,0:T(8,128)S(1)}, u32[]{:S(2)}, u32[]{:S(2)}) async-start(f32[64,80,32]{1,2,0:T(8,128)} %fusion.2), calls=%async_computation | async-start | bytes 2097152 | tf_op jit(solution)/shard_map/all_to_all | solution.py:48
  202.7 0.0 all-reduce.3.cloned.1.call-start
  202.8 0.0 copy-done.1
  202.8 0.1 convert_multiply_fusion
  202.9 0.5 mul.159
  203.4 0.1 cosine_multiply_fusion
  203.5 16.9 %all-to-all-done = f32[64,80,32]{1,2,0:T(8,128)S(1)} async-done(((f32[64,80,32]{1,2,0:T(8,128)}), f32[64,80,32]{1,2,0:T(8,128)S(1)}, u32[]{:S(2)}, u32[]{:S(2)}) %all-to-all-start) | async-done | bytes 655392 | tf_op jit(solution)/shard_map/all_to_all | solution.py:48
  220.4 0.9 multiply_reduce_fusion
  221.3 0.2 dynamic-slice_reduce_fusion
  221.5 145.8 %psum.21 = f32[]{:T(128)} all-reduce(f32[]{:T(128)} %multiply_reduce_fusion), channel_id=1, replica_groups=mesh['dp'=2,'tensor'=64] {'tensor'}, use_global_device_ids=true, to_apply=%region_1.2 | all-reduce | flops 1 | bytes 8 | tf_op jit(solution)/shard_map/psum | solution.py:49
  367.9 0.1 fusion.33
  368.0 3.1 copy.35
  371.1 2.8 mul.160
  373.8 2.5 fusion.5
  376.3 1.0 broadcast_multiply_fusion.2
  377.3 0.0 all-reduce.3.cloned.1.call-update
  377.3 0.1 broadcast_multiply_fusion
  377.4 0.3 copy.34
  377.8 149.1 %all-reduce.3.cloned.1.call-done = f32[8,8,2560]{2,1,0:T(8,128)} async-done(((f32[8,8,2560]{2,1,0:T(8,128)}), f32[8,8,2560]{2,1,0:T(8,128)}) %all-reduce.3.cloned.1.call-update) | async-done | bytes 655376 | tf_op jit(solution)/shard_map/psum | solution.py:57
  526.8 1.8 reshape.114
  528.7 0.0 all-reduce.5.cloned.1.call-start
  528.7 1.8 copy.38
  530.5 0.0 copy-start.2
  530.5 2.3 fusion.26
  532.8 0.0 all-reduce.5.cloned.1.call-update
  532.8 1.1 fusion.8
  533.9 0.3 copy.36
  534.2 0.0 copy-done.2
  534.2 0.8 subtract_convert_fusion
  535.1 22.2 %all-reduce.5.cloned.1.call-done = f32[8,8,2560]{2,1,0:T(8,128)} async-done(((f32[8,8,2560]{2,1,0:T(8,128)}), f32[8,8,2560]{2,1,0:T(8,128)}) %all-reduce.5.cloned.1.call-update) | async-done | bytes 655376 | tf_op jit(solution)/shard_map/psum | solution.py:58
  557.2 1.1 broadcast_multiply_fusion.1
  558.4 0.7 reshape.115
  559.1 1.8 copy.41
  560.9 2.2 fusion.24
  563.1 1.1 convolution_convert_fusion
  564.2 0.9 copy.37
  (2 shorter events, 0.0 us)
Async XLA Ops:
  7.2 152.8 %copy-start = (bf16[2048,32]{0,1:T(8,128)(2,1)S(1)}, bf16[2048,32]{0,1:T(8,128)(2,1)}, u32[]{:S(2)}) copy-start(bf16[2048,32]{0,1:T(8,128)(2,1)} %param.4) | copy-start | bytes 393220
  7.2 124.4 %all-gather.2.cloned.1.call-start = ((), (), s32[]{:S(2)}) async-start(), calls=%async_computation.1 | async-start | bytes 21299200 | tf_op jit(solution)/shard_map/all_gather | solution.py:45
  159.9 42.9 %copy-start.1 = (bf16[1,1,80,2048]{3,2,1,0:T(8,128)(2,1)S(1)}, bf16[1,1,80,2048]{3,2,1,0:T(8,128)(2,1)}, u32[]{:S(2)}) copy-start(bf16[1,1,80,2048]{3,2,1,0:T(8,128)(2,1)} %param.5) | copy-start | bytes 983044
  194.4 26.0 %all-to-all-start = ((f32[64,80,32]{1,2,0:T(8,128)}), f32[64,80,32]{1,2,0:T(8,128)S(1)}, u32[]{:S(2)}, u32[]{:S(2)}) async-start(f32[64,80,32]{1,2,0:T(8,128)} %fusion.2), calls=%async_computation | async-start | bytes 2097152 | tf_op jit(solution)/shard_map/all_to_all | solution.py:48
  202.7 324.1 %all-reduce.3.cloned.1.call-start = ((), (), s32[]{:S(2)}) async-start(), calls=%async_computation.2 | async-start | bytes 1310720 | tf_op jit(solution)/shard_map/psum | solution.py:57
  528.7 28.6 %all-reduce.5.cloned.1.call-start = ((), (), s32[]{:S(2)}) async-start(), calls=%async_computation.3 | async-start | bytes 1310720 | tf_op jit(solution)/shard_map/psum | solution.py:58
  530.5 3.7 copy-start.2
Sparse Core Ops, SparseCore 0:
  10.9 120.6 all-gather.1
  377.5 149.3 all-reduce.2
  532.9 24.2 all-reduce.4
where the time goes:
time: 573 us; the launch traced here: 572 us
  waiting for transfers between devices  313 us (55%)
  blocking collectives  146 us (25%)
  matrix products  43.6 us (8%)
  local copies, waits for them, and re-layouts  42.6 us (7%)
  between operations  14.6 us (3%)
  starting transfers between devices  8.48 us (1%)
    psum x1, waiting for transfers between devices, body(): spectrum = lax.psum(partial_value, 'tensor')  149 us
    psum x1, blocking collectives, body(): squares = lax.psum(jnp.sum(gradient * gradient), 'tensor')  146 us
    all_gather x1, waiting for transfers between devices, body(): block_rows = lax.all_gather(activations, 'tensor', axis=0, tiled=True)  124 us
    dot_general x1, matrix products, body(): jnp.einsum('tan,tc->nac', shaped, head_grads, preferred_element_type=jnp....  34.5 us
    all_gather x1, local copies, waits for them, and re-layouts, body(): block_rows = lax.all_gather(activations, 'tensor', axis=0, tiled=True)  28.4 us
    psum x1, waiting for transfers between devices, body(): replica_total = lax.psum(spectrum, 'dp')  22.2 us
    all_to_all x1, waiting for transfers between devices, body(): lax.all_to_all(by_column, 'tensor', split_axis=0, concat_axis=2, tiled=True)  16.9 us
  transfers between devices with their start and end apart: 4, of which 4 were waited for; matrix products, arithmetic and copies ran while one was open for 1% of the time, Pallas kernels for 0%

commit v1 on v0

v1 whole, which is shorter than its diff:
```python
import math

import jax
import jax.numpy as jnp
import ml_dtypes
import numpy as np
from jax import lax
from jax.experimental import pallas as pl
from jax.experimental.pallas import tpu as pltpu
from jax.sharding import PartitionSpec as P

BLOCK = 64
KEEP = 8
RBLOCKS = 80
COLS = 2048
TOKENS = 2048
LINE = 4
PLANE = 16
ZCOLS = COLS // LINE
ZTOK = TOKENS // LINE
MESH = pl.DeviceIdType.MESH
F32 = jnp.float32
BF16 = jnp.bfloat16
NT = (((1,), (1,)), ((), ()))
TN = (((0,), (0,)), ((), ()))
NN = (((1,), (0,)), ((), ()))


def split(table):
    high = table.astype(np.float32).astype(ml_dtypes.bfloat16)
    low = (table - high.astype(np.float64)).astype(np.float32).astype(ml_dtypes.bfloat16)
    return high, low


def tables():
    k = np.arange(KEEP)[:, None]
    n = np.arange(BLOCK)[None, :]
    scale = np.where(k == 0, math.sqrt(1.0 / BLOCK), math.sqrt(2.0 / BLOCK))
    basis = scale * np.cos(math.pi * (2 * n + 1) * k / (2 * BLOCK))
    sort = np.zeros((256, 256))
    for a in range(4):
        for z in range(LINE):
            for i in range(PLANE):
                sort[a * 64 + z * 16 + i, i * 16 + z * 4 + a] = 1
    pick = np.zeros((LINE * RBLOCKS, 384))
    for tile in range(RBLOCKS // 4):
        for z in range(LINE):
            for a in range(4):
                pick[z * RBLOCKS + 4 * tile + a, tile * 16 + z * 4 + a] = 1
    across = np.kron(np.eye(8), basis)
    order = np.array([z * PLANE + i for i in range(PLANE) for z in range(LINE)])
    project = np.kron((basis.T @ basis)[np.ix_(order, order)], np.eye(4))
    spread_h, spread_l = split(np.kron(np.eye(4), basis))
    spread = np.concatenate([spread_h, spread_h, spread_l], axis=0)
    return (
        sort.astype(ml_dtypes.bfloat16),
        pick.astype(ml_dtypes.bfloat16),
        np.eye(32).astype(ml_dtypes.bfloat16),
        np.stack(split(across)),
        np.stack(split(project)),
        spread,
    )


def dot(a, b, dims):
    return lax.dot_general(a, b, dims, preferred_element_type=F32)


def parts(x):
    high = x.astype(BF16)
    return high, (x - high.astype(F32)).astype(BF16)


def kernel(
    act, head, mom, sort, pick, eye, across, project, spread,
    new_out, upd_out,
    stack, a_send, a_recv, at, gt, grad, grad_row,
    wm_send, wm_recv, pm_send, pm_recv, qm_send, qm_recv, vm, vm_all,
    wg, pg_send, pg_recv, qg_send, qg_recv, vg, vg_all, total_v,
    sa, ra, sz, rz, sg, rg, sgr, rgr, swm, rwm,
    spm, rpm, sqm, rqm, svm, rvm, spg, rpg, sqg, rqg, svg, rvg,
):
    core = lax.axis_index("dp")
    t = lax.axis_index("tensor")
    z, me = lax.div(t, 16), lax.rem(t, 16)
    y, x = lax.div(me, 4), lax.rem(me, 4)

    def shift(v, by):
        return lax.rem(v + by % 4, 4)

    def inplane(d):
        return shift(y, d // 4) * 4 + shift(x, d % 4)

    def copy(src, dst, ssem, rsem, c, zz, ii):
        return pltpu.make_async_remote_copy(
            src_ref=src, dst_ref=dst, send_sem=ssem, recv_sem=rsem,
            device_id=(c, zz * 16 + ii), device_id_type=MESH,
        )

    sent = []

    def go(c):
        c.start()
        sent.append(c)
        return c

    barrier = pltpu.get_barrier_semaphore()
    partners = [(core, z, inplane(d)) for d in range(1, 16)]
    partners += [(core, shift(z, d), me) for d in range(1, 4)]
    partners += [(1 - core, shift(z, d), me) for d in range(4)]
    for c, zz, ii in partners:
        pl.semaphore_signal(barrier, inc=1, device_id=(c, zz * 16 + ii), device_id_type=MESH)
    pl.semaphore_wait(barrier, len(partners))

    for tile in range(20):
        stack[tile * 32:(tile + 1) * 32, :] = act[:, tile * 256:(tile + 1) * 256]
    sorted_cols = dot(stack[...], sort[...], NN)
    group = lax.broadcasted_iota(jnp.int32, (32, 128), 1) // 16
    zero = jnp.zeros((32, 128), F32)
    for half in range(2):
        for octet in range(3):
            v = []
            for tile in range(octet * 8, octet * 8 + 8):
                if tile < 20:
                    v.append(sorted_cols[tile * 32:(tile + 1) * 32, half * 128:(half + 1) * 128])
                else:
                    v.append(zero)
            for d in (1, 2, 4):
                low = (group // d) % 2 == 0
                for k in range(8):
                    if k & d == 0:
                        a, b = v[k], v[k | d]
                        v[k] = jnp.where(low, a, pltpu.roll(b, 16 * d, 1))
                        v[k | d] = jnp.where(low, pltpu.roll(a, 128 - 16 * d, 1), b)
            for k in range(8):
                a_send[half * 8 + k, :, octet * 128:(octet + 1) * 128] = v[k].astype(BF16)
    a_copies = []
    for d in range(1, 16):
        to = inplane(d)
        a_copies.append(go(copy(a_send.at[to], a_recv.at[me], sa.at[d - 1], ra.at[d - 1], core, z, to)))
    a_recv[me] = a_send[me]

    gt[me] = dot(eye[...], head[...], NT).astype(BF16)

    def near(axis, by):
        if axis == 0:
            return y * 4 + shift(x, by)
        return shift(y, by) * 4 + x

    def near2(half, da, db):
        if half == 0:
            return shift(y, db) * 4 + shift(x, da)
        return shift(y, da) * 4 + shift(x, db)

    def g_copy(half, slot, rows, sem, to):
        lanes = pl.ds(half * 1024, 1024)
        where = gt.at[slot, pl.ds(rows[0], rows[1]), lanes]
        return copy(where, where, sg.at[half, sem], rg.at[half, sem], core, z, to)

    whole, upper, lower = (0, 32), (0, 16), (16, 16)

    for half in range(2):
        go(g_copy(half, me, whole, 0, near2(half, 1, 0)))
        go(g_copy(half, me, whole, 1, near2(half, -1, 0)))
    for half in range(2):
        go(g_copy(half, me, whole, 4, near2(half, 0, 1)))
        go(g_copy(half, me, whole, 5, near2(half, 0, -1)))

    wm_send[...] = jnp.zeros_like(wm_send)
    wg[...] = jnp.zeros_like(wg)
    for zz in range(LINE):
        piece = mom[:, zz * ZCOLS:(zz + 1) * ZCOLS]
        wm_send[zz, :, 0:RBLOCKS] = dot(across[0], piece, NT) + dot(across[1], piece, NT)
    wm_copies = []
    for d in range(1, 4):
        to = shift(z, d)
        wm_copies.append(go(copy(wm_send.at[to], wm_recv.at[z], swm.at[d - 1], rwm.at[d - 1], core, to, me)))
    wm_recv[z] = wm_send[z]

    def g_wait_from(half, da, db, rows, sem, to):
        g_copy(half, near2(half, da, db), rows, sem, to).wait_recv()

    for half in range(2):
        g_wait_from(half, -1, 0, whole, 0, near2(half, 1, 0))
        go(g_copy(half, near2(half, -1, 0), upper, 2, near2(half, 1, 0)))
        g_wait_from(half, 1, 0, whole, 1, near2(half, -1, 0))
        go(g_copy(half, near2(half, 1, 0), lower, 3, near2(half, -1, 0)))
    for half in range(2):
        for j, da in ((1, -1), (2, 1)):
            go(g_copy(half, near2(half, da, 0), whole, 4 + 4 * j, near2(half, 0, 1)))
            go(g_copy(half, near2(half, da, 0), whole, 5 + 4 * j, near2(half, 0, -1)))

    for c in a_copies:
        c.wait_recv()
    at[z] = dot(pick[...], a_recv[...].reshape(ZTOK, 384), NT).astype(BF16)

    def z_copy(slot, rows, sem, to):
        where = at.at[slot, pl.ds(rows[0], rows[1]), :]
        return copy(where, where, sz.at[sem], rz.at[sem], core, to, me)

    every, first, second = (0, 320), (0, 160), (160, 160)
    zu, zd, zo = shift(z, 1), shift(z, -1), shift(z, 2)
    go(z_copy(z, every, 0, zu))
    go(z_copy(z, every, 1, zd))

    def regroup_w(src, dst):
        for q in range(PLANE):
            for zz in range(LINE):
                dst[q, 4 * zz:4 * zz + 4, :] = src[zz, 4 * q:4 * q + 4, :]

    def regroup_v(src, dst):
        for q in range(PLANE):
            for zz in range(LINE):
                dst[zz, 4 * q:4 * q + 4, :] = src[q, 4 * zz:4 * zz + 4, :]

    def plane_start(src, dst, ssem, rsem):
        out = []
        for d in range(1, 16):
            to = inplane(d)
            out.append(go(copy(src.at[to], dst.at[me], ssem.at[d - 1], rsem.at[d - 1], core, z, to)))
        dst[me] = src[me]
        return out

    def line_start(src, dst, ssem, rsem):
        out = []
        for d in range(4):
            to = shift(z, d)
            if d > 0:
                out.append(go(copy(src.at[to], dst.at[core, z], ssem.at[0, d], rsem.at[0, d], core, to, me)))
            out.append(go(copy(src.at[to], dst.at[core, z], ssem.at[1, d], rsem.at[1, d], 1 - core, to, me)))
        dst[core, z] = src[z]
        return out

    def apply_project(w):
        high, low = parts(w)
        return dot(project[0], high, NN) + dot(project[0], low, NN) + dot(project[1], high, NN)

    for c in wm_copies:
        c.wait_recv()
    regroup_w(wm_recv, pm_send)
    pm_copies = plane_start(pm_send, pm_recv, spm, rpm)

    for half in range(2):
        g_wait_from(half, 2, 0, upper, 2, near2(half, 1, 0))
        g_wait_from(half, 2, 0, lower, 3, near2(half, -1, 0))
        go(g_copy(half, near2(half, 2, 0), whole, 16, near2(half, 0, 1)))
        go(g_copy(half, near2(half, 2, 0), whole, 17, near2(half, 0, -1)))
    for j, da in ((0, 0), (1, -1), (2, 1)):
        for half in range(2):
            g_wait_from(half, da, -1, whole, 4 + 4 * j, near2(half, 0, 1))
            go(g_copy(half, near2(half, da, -1), upper, 6 + 4 * j, near2(half, 0, 1)))
            g_wait_from(half, da, 1, whole, 5 + 4 * j, near2(half, 0, -1))
            go(g_copy(half, near2(half, da, 1), lower, 7 + 4 * j, near2(half, 0, -1)))

    for c in pm_copies:
        c.wait_recv()
    qm_send[...] = apply_project(pm_recv[...].reshape(256, 128)).reshape(PLANE, 16, 128)
    qm_copies = plane_start(qm_send, qm_recv, sqm, rqm)

    z_copy(zd, every, 0, zu).wait_recv()
    go(z_copy(zd, first, 2, zu))
    z_copy(zu, every, 1, zd).wait_recv()
    go(z_copy(zu, second, 3, zd))

    for half in range(2):
        g_wait_from(half, 2, -1, whole, 16, near2(half, 0, 1))
        go(g_copy(half, near2(half, 2, -1), upper, 18, near2(half, 0, 1)))
        g_wait_from(half, 2, 1, whole, 17, near2(half, 0, -1))
        go(g_copy(half, near2(half, 2, 1), lower, 19, near2(half, 0, -1)))

    for c in qm_copies:
        c.wait_recv()
    regroup_v(qm_recv, vm)
    vm_copies = line_start(vm, vm_all, svm, rvm)

    for j, da in ((0, 0), (1, -1), (2, 1), (3, 2)):
        for half in range(2):
            g_wait_from(half, da, 2, upper, 6 + 4 * j, near2(half, 0, 1))
            g_wait_from(half, da, 2, lower, 7 + 4 * j, near2(half, 0, -1))
    z_copy(zo, first, 2, zu).wait_recv()
    z_copy(zo, second, 3, zd).wait_recv()

    acc = None
    for zz in range(LINE):
        term = dot(at[zz], gt[:, :, zz * ZTOK:(zz + 1) * ZTOK].reshape(ZCOLS, ZTOK), NT)
        acc = term if acc is None else acc + term
    grad[...] = acc.reshape(LINE, RBLOCKS, ZCOLS)
    grad_copies = []
    for d in range(1, 4):
        to = shift(z, d)
        grad_copies.append(go(copy(grad.at[to], grad_row.at[z], sgr.at[d - 1], rgr.at[d - 1], core, to, me)))
    grad_row[z] = grad[z]
    for zz in range(LINE):
        high, low = parts(grad[zz])
        wg[zz, :, 0:RBLOCKS] = (
            dot(across[0], high, NT) + dot(across[0], low, NT) + dot(across[1], high, NT)
        )
    squares = jnp.zeros((8, 128), F32)
    for zz in range(LINE):
        piece = grad[zz]
        sq = piece * piece
        for lane in range(4):
            squares += jnp.sum(sq[:, lane * 128:(lane + 1) * 128].reshape(10, 8, 128), axis=0)
    regroup_w(wg, pg_send)
    for q in range(PLANE):
        pg_send[q, 16:24, :] = squares
    pg_copies = plane_start(pg_send, pg_recv, spg, rpg)
    for c in pg_copies:
        c.wait_recv()
    qg_send[...] = apply_project(pg_recv[:, 0:16, :].reshape(256, 128)).reshape(PLANE, 16, 128)
    qg_copies = plane_start(qg_send, qg_recv, sqg, rqg)
    plane_sq = jnp.sum(pg_recv[:, 16:24, :], axis=0)
    for zz in range(LINE):
        vg[zz, 64:72, :] = plane_sq
    for c in qg_copies:
        c.wait_recv()
    regroup_v(qg_recv, vg)
    vg_copies = line_start(vg, vg_all, svg, rvg)
    for c in vm_copies:
        c.wait_recv()
    for c in vg_copies:
        c.wait_recv()

    factors = []
    for r in range(2):
        square = vg_all[r, 0, 64:72, :]
        for zz in range(1, LINE):
            square = square + vg_all[r, zz, 64:72, :]
        square = jnp.sum(jnp.sum(square, axis=0, keepdims=True), axis=1, keepdims=True)
        factors.append(jnp.minimum(F32(1.0), 1.0 / jnp.sqrt(square / (RBLOCKS * BLOCK * COLS) + 1e-06)))
        for zz in range(LINE):
            total_v[r, zz * 64:(zz + 1) * 64, :] = (
                F32(0.9) * vm_all[r, zz] + factors[r] * vg_all[r, zz, 0:64, :]
            )
    factor = jnp.where(core == 0, factors[0], factors[1])

    def kept(v):
        high, low = parts(v)
        return dot(jnp.concatenate([high, low, high], axis=0), spread[...], TN)[0:RBLOCKS]

    for g in range(8):
        rows = slice(g * 32, (g + 1) * 32)
        cols = slice(g * 256, (g + 1) * 256)
        both = (total_v[0, rows, :] + total_v[1, rows, :]) * F32(0.5)
        upd_out[:, cols] = kept(both).astype(BF16)
    for c in grad_copies:
        c.wait_recv()
    for g in range(8):
        rows = slice(g * 32, (g + 1) * 32)
        cols = slice(g * 256, (g + 1) * 256)
        local = slice((g % 2) * 256, (g % 2) * 256 + 256)
        full = F32(0.9) * mom[:, cols].astype(F32) + factor * grad_row[g // 2, :, local]
        new_out[:, cols] = (full - kept(total_v[core, rows, :])).astype(BF16)
    for c in sent:
        c.wait_send()


def body(activations, head_grads, momentum):
    dma = pltpu.SemaphoreType.DMA
    consts = [jnp.asarray(c) for c in tables()]
    vmem = pl.BlockSpec(memory_space=pltpu.VMEM)
    scratch = [
        pltpu.VMEM((640, 256), BF16),
        pltpu.VMEM((PLANE, 32, 384), BF16),
        pltpu.VMEM((PLANE, 32, 384), BF16),
        pltpu.VMEM((LINE, 320, ZTOK), BF16),
        pltpu.VMEM((PLANE, 32, TOKENS), BF16),
        pltpu.VMEM((LINE, RBLOCKS, ZCOLS), F32),
        pltpu.VMEM((LINE, RBLOCKS, ZCOLS), F32),
        pltpu.VMEM((LINE, 64, 128), F32),
        pltpu.VMEM((LINE, 64, 128), F32),
        pltpu.VMEM((PLANE, 16, 128), F32),
        pltpu.VMEM((PLANE, 16, 128), F32),
        pltpu.VMEM((PLANE, 16, 128), F32),
        pltpu.VMEM((PLANE, 16, 128), F32),
        pltpu.VMEM((LINE, 64, 128), F32),
        pltpu.VMEM((2, LINE, 64, 128), F32),
        pltpu.VMEM((LINE, 64, 128), F32),
        pltpu.VMEM((PLANE, 24, 128), F32),
        pltpu.VMEM((PLANE, 24, 128), F32),
        pltpu.VMEM((PLANE, 16, 128), F32),
        pltpu.VMEM((PLANE, 16, 128), F32),
        pltpu.VMEM((LINE, 72, 128), F32),
        pltpu.VMEM((2, LINE, 72, 128), F32),
        pltpu.VMEM((2, 256, 128), F32),
    ]
    for shape in ((15,), (4,), (2, 20), (3,), (3,), (15,), (15,), (2, 4), (15,), (15,), (2, 4)):
        scratch += [dma(shape), dma(shape)]
    new, upd = pl.pallas_call(
        kernel,
        out_shape=(
            jax.ShapeDtypeStruct((RBLOCKS, COLS), BF16),
            jax.ShapeDtypeStruct((RBLOCKS, COLS), BF16),
        ),
        in_specs=[vmem] * 9,
        out_specs=(vmem, vmem),
        scratch_shapes=scratch,
        compiler_params=pltpu.CompilerParams(
            collective_id=0, has_side_effects=True, vmem_limit_bytes=40 * 1024 * 1024
        ),
    )(activations, head_grads, momentum.reshape(RBLOCKS, COLS), *consts)
    return new[None, None], upd[None]


def solution(mesh):
    placed = (P(("dp", "tensor"), None), P("dp", "tensor"), P("dp", "tensor", None, None))
    return jax.shard_map(
        body,
        mesh=mesh,
        in_specs=placed,
        out_specs=(P("dp", "tensor", None, None), P("tensor", None, None)),
        check_vma=False,
    )
```

time: 573 us -> 64.6 us (0.11)
  waiting for transfers between devices: 313 us -> 0 us
  blocking collectives: 146 us -> 0 us
  Pallas kernels: 0 us -> 55.7 us
  matrix products: 43.6 us -> 0 us
  local copies, waits for them, and re-layouts: 42.6 us -> 7.89 us
  between operations: 14.6 us -> 0.69 us
  starting transfers between devices: 8.48 us -> 0 us
    psum x2 -> x0, waiting for transfers between devices: 171 us -> none  [the longest x1 149 us: body(): spectrum = lax.psum(partial_value, 'tensor')]
    psum x1 -> x0, blocking collectives: 146 us -> none  [body(): squares = lax.psum(jnp.sum(gradient * gradient), 'tensor')]
    all_gather x1 -> x0, waiting for transfers between devices: 124 us -> none  [body(): block_rows = lax.all_gather(activations, 'tensor', axis=0, tiled=True)]
    pallas_call x0 -> x1, Pallas kernels: none -> 55.7 us  [body(): pl.pallas_call(kernel, out_shape=(jax.ShapeDtypeStruct((RBLOCKS, COLS), B...]
    dot_general x6 -> x0, matrix products: 43.6 us -> none  [the longest x1 34.5 us: body(): jnp.einsum('tan,tc->nac', shaped, head_grads, preferred_element_type=jnp....]
    all_gather x1 -> x0, local copies, waits for them, and re-layouts: 28.4 us -> none  [body(): block_rows = lax.all_gather(activations, 'tensor', axis=0, tiled=True)]
    all_to_all x1 -> x0, waiting for transfers between devices: 16.9 us -> none  [body(): lax.all_to_all(by_column, 'tensor', split_axis=0, concat_axis=2, tiled=True)]
    all_to_all x1 -> x0, starting transfers between devices: 8.36 us -> none  [body(): lax.all_to_all(by_column, 'tensor', split_axis=0, concat_axis=2, tiled=True)]
  transfers between devices with their start and end apart: 4 -> 0, of which waited for: 4 -> 0; matrix products, arithmetic and copies ran while one was open for 1% -> 0% of each run, Pallas kernels for 0% -> 0%
where the time goes in v1:
time: 64.6 us; the launch traced here: 64.3 us
  Pallas kernels  55.7 us (86%)
  local copies, waits for them, and re-layouts  7.89 us (12%)
  between operations  0.69 us (1%)
    pallas_call x1, Pallas kernels, body(): pl.pallas_call(kernel, out_shape=(jax.ShapeDtypeStruct((RBLOCKS, COLS), B...  55.7 us
    unnamed x19, local copies, waits for them, and re-layouts  7.89 us

profile of v1, /device:TPU:1, one launch (start us, length us, event | category | flops | bytes accessed | tf_op | source)
XLA Modules:
  0.0 64.3 jit_solution(4715524628324027733)
XLA Ops:
  0.6 0.0 copy-start
  0.6 0.0 copy-start.1
  0.6 1.2 %copy.11.head = bf16[2048,32]{1,0:T(8,128)(2,1)S(1)} copy(bf16[2048,32]{0,1:T(8,128)(2,1)} %param.10) | data formatting | bytes 262144 | tf_op args[1]
  1.9 0.0 copy-done
  1.9 0.0 copy-done.1
  1.9 0.0 copy-start.2
  1.9 0.9 %copy-done.2 = bf16[2,256,256]{2,1,0:T(8,128)(2,1)S(1)} copy-done((bf16[2,256,256]{2,1,0:T(8,128)(2,1)S(1)}, bf16[2,256,256]{2,1,0:T(8,128)(2,1)}, u32[]{:S(2)}) %copy-start.2) | copy-done | bytes 262168
  2.9 0.0 copy-start.3
  2.9 0.9 %copy-done.3 = bf16[320,384]{1,0:T(8,128)(2,1)S(1)} copy-done((bf16[320,384]{1,0:T(8,128)(2,1)S(1)}, bf16[320,384]{1,0:T(8,128)(2,1)}, u32[]{:S(2)}) %copy-start.3) | copy-done | bytes 245784
  3.8 0.0 copy-start.4
  3.8 0.9 %copy-done.4 = bf16[2,64,512]{2,1,0:T(8,128)(2,1)S(1)} copy-done((bf16[2,64,512]{2,1,0:T(8,128)(2,1)S(1)}, bf16[2,64,512]{2,1,0:T(8,128)(2,1)}, u32[]{:S(2)}) %copy-start.4) | copy-done | bytes 131096
  4.7 0.0 copy-start.5
  4.7 0.9 %copy-done.5 = bf16[256,256]{1,0:T(8,128)(2,1)S(1)} copy-done((bf16[256,256]{1,0:T(8,128)(2,1)S(1)}, bf16[256,256]{1,0:T(8,128)(2,1)}, u32[]{:S(2)}) %copy-start.5) | copy-done | bytes 131096
  5.6 0.0 copy-start.6
  5.6 0.8 %copy-done.6 = bf16[96,256]{1,0:T(8,128)(2,1)S(1)} copy-done((bf16[96,256]{1,0:T(8,128)(2,1)S(1)}, bf16[96,256]{1,0:T(8,128)(2,1)}, u32[]{:S(2)}) %copy-start.6) | copy-done | bytes 49176
  6.4 0.0 copy-start.7
  6.4 0.7 %copy-done.7 = bf16[32,32]{1,0:T(8,128)(2,1)S(1)} copy-done((bf16[32,32]{1,0:T(8,128)(2,1)S(1)}, bf16[32,32]{1,0:T(8,128)(2,1)}, u32[]{:S(2)}) %copy-start.7) | copy-done | bytes 2072
  7.1 55.7 %shard_map.104 = (bf16[80,2048]{1,0:T(8,128)(2,1)S(1)}, bf16[80,2048]{1,0:T(8,128)(2,1)S(1)}) custom-call(bf16[32,5120]{1,0:T(8,128)(2,1)S(1)} %copy-done, bf16[2048,32]{1,0:T(8,128)(2,1)S(1)} %copy.11.head, bf16[80,2048]{1,0:T(8,128)(2,1)S(1)} %bitcast.5, bf16[256,256]{1,0:T(8,128)(2,1)S(1)} %copy-done.5, bf16[320,384]{1,0:T(8,128)(2,1)S(1)} %copy-done.3, ...), custom_call_target="tpu_custom_call" | custom-call | tf_op jit(solution)/shard_map/pallas_call | solution.py:389
  62.8 0.7 %copy.14 = bf16[1,1,80,2048]{3,2,1,0:T(8,128)(2,1)} copy(bf16[1,1,80,2048]{3,2,1,0:T(8,128)(2,1)S(1)} %bitcast.4) | data formatting | bytes 655360
  63.5 0.7 %copy.15 = bf16[1,80,2048]{2,1,0:T(8,128)(2,1)} copy(bf16[1,80,2048]{2,1,0:T(8,128)(2,1)S(1)} %bitcast.3) | data formatting | bytes 655360
Async XLA Ops:
  0.6 1.3 %copy-start = (bf16[32,5120]{1,0:T(8,128)(2,1)S(1)}, bf16[32,5120]{1,0:T(8,128)(2,1)}, u32[]{:S(2)}) copy-start(bf16[32,5120]{1,0:T(8,128)(2,1)} %act.1) | copy-start | bytes 983044
  0.6 1.3 %copy-start.1 = (bf16[1,1,80,2048]{3,2,1,0:T(8,128)(2,1)S(1)}, bf16[1,1,80,2048]{3,2,1,0:T(8,128)(2,1)}, u32[]{:S(2)}) copy-start(bf16[1,1,80,2048]{3,2,1,0:T(8,128)(2,1)} %param.11) | copy-start | bytes 983044
  1.9 1.0 %copy-start.2 = (bf16[2,256,256]{2,1,0:T(8,128)(2,1)S(1)}, bf16[2,256,256]{2,1,0:T(8,128)(2,1)}, u32[]{:S(2)}) copy-start(bf16[2,256,256]{2,1,0:T(8,128)(2,1)} %constant.16.clone.project) | copy-start | bytes 786436
  2.9 0.9 %copy-start.3 = (bf16[320,384]{1,0:T(8,128)(2,1)S(1)}, bf16[320,384]{1,0:T(8,128)(2,1)}, u32[]{:S(2)}) copy-start(bf16[320,384]{1,0:T(8,128)(2,1)} %constant.13.clone.pick) | copy-start | bytes 737284
  3.8 0.9 %copy-start.4 = (bf16[2,64,512]{2,1,0:T(8,128)(2,1)S(1)}, bf16[2,64,512]{2,1,0:T(8,128)(2,1)}, u32[]{:S(2)}) copy-start(bf16[2,64,512]{2,1,0:T(8,128)(2,1)} %constant.15.clone.across) | copy-start | bytes 393220
  4.7 0.9 %copy-start.5 = (bf16[256,256]{1,0:T(8,128)(2,1)S(1)}, bf16[256,256]{1,0:T(8,128)(2,1)}, u32[]{:S(2)}) copy-start(bf16[256,256]{1,0:T(8,128)(2,1)} %constant.12.clone.sort) | copy-start | bytes 393220
  5.6 0.8 %copy-start.6 = (bf16[96,256]{1,0:T(8,128)(2,1)S(1)}, bf16[96,256]{1,0:T(8,128)(2,1)}, u32[]{:S(2)}) copy-start(bf16[96,256]{1,0:T(8,128)(2,1)} %constant.17.clone.spread) | copy-start | bytes 147460
  6.4 0.7 %copy-start.7 = (bf16[32,32]{1,0:T(8,128)(2,1)S(1)}, bf16[32,32]{1,0:T(8,128)(2,1)}, u32[]{:S(2)}) copy-start(bf16[32,32]{1,0:T(8,128)(2,1)} %constant.14.clone.eye) | copy-start | bytes 6148

commit v2 on v1

v2 whole, which is shorter than its diff:
```python
import math

import jax
import jax.numpy as jnp
import ml_dtypes
import numpy as np
from jax import lax
from jax.experimental import pallas as pl
from jax.experimental.pallas import tpu as pltpu
from jax.sharding import PartitionSpec as P

BLOCK = 64
KEEP = 8
RBLOCKS = 80
COLS = 2048
TOKENS = 2048
LINE = 4
PLANE = 16
ZCOLS = COLS // LINE
ZTOK = TOKENS // LINE
MESH = pl.DeviceIdType.MESH
F32 = jnp.float32
BF16 = jnp.bfloat16
NT = (((1,), (1,)), ((), ()))
TN = (((0,), (0,)), ((), ()))
NN = (((1,), (0,)), ((), ()))
ORDER = ("a0", "a1", "a3", "s", "a2", "g0", "z0", "f", "z1", "z3", "g1", "g2", "z2", "g3", "m1")
START = "A12"
MSTEPS = ((2,), (3, 4))
AORD = (1, 3, 2, 4, 12, 5, 7, 13, 15, 6, 14, 8, 9, 11, 10)


def split(table):
    high = table.astype(np.float32).astype(ml_dtypes.bfloat16)
    low = (table - high.astype(np.float64)).astype(np.float32).astype(ml_dtypes.bfloat16)
    return high, low


def tables():
    k = np.arange(KEEP)[:, None]
    n = np.arange(BLOCK)[None, :]
    scale = np.where(k == 0, math.sqrt(1.0 / BLOCK), math.sqrt(2.0 / BLOCK))
    basis = scale * np.cos(math.pi * (2 * n + 1) * k / (2 * BLOCK))
    sort = np.zeros((256, 256))
    for a in range(4):
        for z in range(LINE):
            for i in range(PLANE):
                sort[a * 64 + z * 16 + i, i * 16 + z * 4 + a] = 1
    pick = np.zeros((LINE * RBLOCKS, 384))
    for tile in range(RBLOCKS // 4):
        for z in range(LINE):
            for a in range(4):
                pick[z * RBLOCKS + 4 * tile + a, tile * 16 + z * 4 + a] = 1
    across = np.kron(np.eye(8), basis)
    order = np.array([z * PLANE + i for i in range(PLANE) for z in range(LINE)])
    project = np.kron((basis.T @ basis)[np.ix_(order, order)], np.eye(4))
    gather_n = np.kron(basis[:, order], np.eye(4))
    back = np.zeros((BLOCK, 2, 4, 2, KEEP, 4))
    spread = np.zeros((2, 4, 2, 2, 4, 2, 4, BLOCK))
    for r in range(2):
        for l in range(4):
            back[:, r, l, r, :, l] = basis.T
        for b in range(4):
            for half in range(2):
                rows = basis[half * 4:half * 4 + 4]
                spread[r, b, half, r, :, 0, b] = rows
                spread[:, b, half, r, :, 1, b] = 0.5 * rows
    back_h, back_l = split(back.reshape(512, 64))
    back = np.concatenate([back_h, back_h, back_l], axis=1)
    spread_h, spread_l = split(spread.reshape(2, 64, 512))
    spread = np.concatenate([spread_h, spread_h, spread_l], axis=1)
    return (
        sort.astype(ml_dtypes.bfloat16),
        pick.astype(ml_dtypes.bfloat16),
        np.concatenate(split(across), axis=0),
        np.stack(split(project)),
        np.concatenate(split(gather_n), axis=0),
        back,
        spread,
    )


def dot(a, b, dims):
    return lax.dot_general(a, b, dims, preferred_element_type=F32)


def parts(x):
    high = x.astype(BF16)
    return high, (x - high.astype(F32)).astype(BF16)


def kernel(
    act_hbm, head_hbm, mom_hbm, sort_hbm, pick_hbm, across_hbm, project_hbm, keep_hbm, back_hbm, spread_hbm,
    new_out, upd_out,
    act, mom, sort, pick, across, project, keep, back, spread, stack,
    a_send, a_recv, at, gt, grad, grad_row,
    wm_send, wm_recv, pm_send, pm_recv, qm_send, qm_recv, vm, vm_all,
    wg, pg_send, pg_recv, coef, vg, vg_all, vm_rows, total_v,
    load, sa, ra, sz, rz, sg, rg, sgr, rgr, swm, rwm,
    spm, rpm, sqm, rqm, svm, rvm, spg, rpg, sqg, rqg, sfg, rfg,
):
    core = lax.axis_index("dp")
    t = lax.axis_index("tensor")
    z, me = lax.div(t, 16), lax.rem(t, 16)
    y, x = lax.div(me, 4), lax.rem(me, 4)

    def shift(v, by):
        return lax.rem(v + by % 4, 4)

    def inplane(d):
        return shift(y, d // 4) * 4 + shift(x, d % 4)

    def hops(dz, d):
        return sum(min(v, 4 - v) for v in (dz, d // 4, d % 4))

    far_first = sorted(range(1, 16), key=lambda d: -hops(0, d))

    def copy(src, dst, ssem, rsem, c, zz, ii):
        return pltpu.make_async_remote_copy(
            src_ref=src, dst_ref=dst, send_sem=ssem, recv_sem=rsem,
            device_id=(c, zz * 16 + ii), device_id_type=MESH,
        )

    sent = []
    arrived = set()

    def go(c):
        c.start()
        sent.append(c)
        return c

    def wait(c):
        c.wait_recv()
        arrived.add(id(c))

    barrier = pltpu.get_barrier_semaphore()
    partners = [(core, z, inplane(d)) for d in far_first]
    partners += [(core, shift(z, d), me) for d in (2, 1, 3)] + [(1 - core, z, me)]
    for c, zz, ii in partners:
        pl.semaphore_signal(barrier, inc=1, device_id=(c, zz * 16 + ii), device_id_type=MESH)

    loads = {}
    for k, (name, src, dst) in enumerate((
        ("act", act_hbm, act), ("sort", sort_hbm, sort), ("head", head_hbm, gt.at[me]),
        ("mom", mom_hbm, mom), ("pick", pick_hbm, pick), ("across", across_hbm, across),
        ("project", project_hbm, project), ("keep", keep_hbm, keep), ("back", back_hbm, back), ("spread", spread_hbm, spread),
    )):
        loads[name] = pltpu.make_async_copy(src, dst, load.at[k])
        loads[name].start()

    loads["act"].wait()
    loads["sort"].wait()
    for tile in range(20):
        stack[tile * 32:(tile + 1) * 32, :] = act[:, tile * 256:(tile + 1) * 256]
    sorted_cols = dot(stack[...], sort[...], NN)
    group = lax.broadcasted_iota(jnp.int32, (32, 128), 1) // 16
    zero = jnp.zeros((32, 128), F32)
    for half in range(2):
        for octet in range(3):
            v = []
            for tile in range(octet * 8, octet * 8 + 8):
                if tile < 20:
                    v.append(sorted_cols[tile * 32:(tile + 1) * 32, half * 128:(half + 1) * 128])
                else:
                    v.append(zero)
            for d in (1, 2, 4):
                low = (group // d) % 2 == 0
                for k in range(8):
                    if k & d == 0:
                        a, b = v[k], v[k | d]
                        v[k] = jnp.where(low, a, pltpu.roll(b, 16 * d, 1))
                        v[k | d] = jnp.where(low, pltpu.roll(a, 128 - 16 * d, 1), b)
            for k in range(8):
                a_send[half * 8 + k, :, octet * 128:(octet + 1) * 128] = v[k].astype(BF16)

    pl.semaphore_wait(barrier, len(partners))

    loads["head"].wait()

    def near2(half, da, db):
        if half == 0:
            return shift(y, db) * 4 + shift(x, da)
        return shift(y, da) * 4 + shift(x, db)

    g_copies = {}

    def g_go(half, slot, rows, sem, to):
        lanes = pl.ds(half * 1024, 1024)
        where = gt.at[slot, pl.ds(rows[0], rows[1]), lanes]
        g_copies[half, sem] = go(copy(where, where, sg.at[half, sem], rg.at[half, sem], core, z, to))

    def g_wait(half, sem):
        wait(g_copies[half, sem])

    whole, upper, lower = (0, 32), (0, 16), (16, 16)

    a_copies = {}
    def start_a(offsets):
        for d in offsets:
            to = inplane(d)
            a_copies[d] = go(copy(a_send.at[to], a_recv.at[me], sa.at[d - 1], ra.at[d - 1], core, z, to))

    def start_g1():
        for half in range(2):
            g_go(half, me, whole, 0, near2(half, 1, 0))
            g_go(half, me, whole, 1, near2(half, -1, 0))

    def start_g2():
        for half in range(2):
            g_go(half, me, whole, 4, near2(half, 0, 1))
            g_go(half, me, whole, 5, near2(half, 0, -1))


    a_recv[me] = a_send[me]
    for step in START:
        {"A": lambda: start_a(AORD), "1": start_g1, "2": start_g2}[step]()

    def dot_across(piece):
        both = dot(across[...], piece, NT)
        return both[0:64] + both[64:128]

    for name in ("mom", "across", "pick", "project", "keep", "back", "spread"):
        loads[name].wait()
    wm_send[...] = jnp.zeros_like(wm_send)
    wg[...] = jnp.zeros_like(wg)
    for zz in range(LINE):
        piece = mom[:, zz * ZCOLS:(zz + 1) * ZCOLS]
        wm_send[zz, :, 0:RBLOCKS] = dot_across(piece)
    wm_copies = []

    def wm_start():
        for d in range(1, 4):
            to = shift(z, d)
            wm_copies.append(go(copy(wm_send.at[to], wm_recv.at[z], swm.at[d - 1], rwm.at[d - 1], core, to, me)))
        wm_recv[z] = wm_send[z]

    wm_start()

    z_copies = {}
    zu, zd, zo = shift(z, 1), shift(z, -1), shift(z, 2)
    every, first, second = (0, 320), (0, 160), (160, 160)

    def z_go(slot, dy, rows, sem, to):
        where = at.at[slot, shift(y, dy), pl.ds(rows[0], rows[1]), :]
        z_copies[dy, sem] = go(copy(where, where, sz.at[dy, sem], rz.at[dy, sem], core, to, me))

    def z_wait(dy, sem):
        wait(z_copies[dy, sem])

    def a_line(dy):
        for dx in range(4):
            d = (-dy % 4) * 4 + (-dx % 4)
            if d:
                wait(a_copies[d])
        line = shift(y, dy)
        tokens = a_recv[pl.ds(line * 4, 4)].reshape(128, 384)
        at[z, line] = dot(pick[...], tokens, NT).astype(BF16)
        z_go(z, dy, every, 0, zu)
        z_go(z, dy, every, 1, zd)

    def z_relay(dy):
        z_wait(dy, 0)
        z_go(zd, dy, first, 2, zu)
        z_wait(dy, 1)
        z_go(zu, dy, second, 3, zd)

    def g_relay(j, da):
        for half in range(2):
            g_wait(half, 4 + 4 * j)
            g_go(half, near2(half, da, -1), upper, 6 + 4 * j, near2(half, 0, 1))
            g_wait(half, 5 + 4 * j)
            g_go(half, near2(half, da, 1), lower, 7 + 4 * j, near2(half, 0, -1))

    def regroup_w(src, dst):
        for q in range(PLANE):
            for zz in range(LINE):
                dst[q, 4 * zz:4 * zz + 4, :] = src[zz, 4 * q:4 * q + 4, :]

    def regroup_v(src, dst):
        for q in range(PLANE):
            for zz in range(LINE):
                dst[zz, 4 * q:4 * q + 4, :] = src[q, 4 * zz:4 * zz + 4, :]

    def plane_start(src, dst, ssem, rsem):
        out = []
        for d in far_first:
            to = inplane(d)
            out.append(go(copy(src.at[to], dst.at[me], ssem.at[d - 1], rsem.at[d - 1], core, z, to)))
        dst[me] = src[me]
        return out

    def line_start(src, dst, ssem, rsem):
        out = {0: go(copy(src.at[z], dst.at[core, z], ssem.at[1, 0], rsem.at[1, 0], 1 - core, z, me))}
        for d in (2, 1, 3):
            to = shift(z, d)
            out[d] = go(copy(src.at[to], dst.at[core, z], ssem.at[0, d], rsem.at[0, d], core, to, me))
        dst[core, z] = src[z]
        return out

    def line_end(out, dst, ssem, rsem):
        forward = [out[0]]
        for d in (1, 3, 2):
            wait(out[d])
            where = dst.at[core, shift(z, -d)]
            forward.append(go(copy(where, where, ssem.at[1, d], rsem.at[1, d], 1 - core, z, me)))
        return forward

    def apply_project(w):
        high, low = parts(w)
        return dot(project[0], high, NN) + dot(project[0], low, NN) + dot(project[1], high, NN)

    pm_copies, qm_copies, vm_copies = [], [], []

    def momentum_step(which):
        if which == 1:
            for c in wm_copies:
                wait(c)
            regroup_w(wm_recv, pm_send)
            pm_copies.extend(plane_start(pm_send, pm_recv, spm, rpm))
        elif which == 2:
            for c in pm_copies:
                wait(c)
            qm_send[...] = apply_project(pm_recv[...].reshape(256, 128)).reshape(PLANE, 16, 128)
            qm_copies.extend(plane_start(qm_send, qm_recv, sqm, rqm))
        elif which == 3:
            for c in qm_copies:
                wait(c)
            regroup_v(qm_recv, vm)
            vm_copies.append(line_start(vm, vm_all, svm, rvm))
        else:
            for c in line_end(vm_copies[0], vm_all, svm, rvm):
                wait(c)
            for r in range(2):
                for zz in range(LINE):
                    for q in range(PLANE):
                        vm_rows[zz * 16 + q, 4 * r:4 * r + 4, :] = vm_all[r, zz, 4 * q:4 * q + 4, :]

    def near_chunks():
        for half in range(2):
            g_wait(half, 0)
            g_go(half, near2(half, -1, 0), upper, 2, near2(half, 1, 0))
            g_wait(half, 1)
            g_go(half, near2(half, 1, 0), lower, 3, near2(half, -1, 0))
        for half in range(2):
            for j, da in ((1, -1), (2, 1)):
                g_go(half, near2(half, da, 0), whole, 4 + 4 * j, near2(half, 0, 1))
                g_go(half, near2(half, da, 0), whole, 5 + 4 * j, near2(half, 0, -1))

    def far_chunk():
        for half in range(2):
            g_wait(half, 2)
            g_wait(half, 3)
            g_go(half, near2(half, 2, 0), whole, 16, near2(half, 0, 1))
            g_go(half, near2(half, 2, 0), whole, 17, near2(half, 0, -1))

    for step in ORDER:
        kind, which = step[0], step[1:]
        if kind == "a":
            a_line(int(which))
        elif kind == "z":
            z_relay(int(which))
        elif kind == "s":
            near_chunks()
        elif kind == "f":
            far_chunk()
        elif kind == "m":
            momentum_step(int(which))
        else:
            g_relay(int(which), (0, -1, 1, 2)[int(which)])

    for j in range(4):
        for half in range(2):
            g_wait(half, 6 + 4 * j)
            g_wait(half, 7 + 4 * j)
    for dy in (0, 1, 3, 2):
        z_wait(dy, 2)
        z_wait(dy, 3)

    grad_copies, pg_copies, qg_copies, vg_copies = [], [], [], []
    acc = None
    for zz in range(LINE):
        left = jnp.concatenate([at[zz, yy] for yy in range(4)], axis=1)
        term = dot(left, gt[:, :, zz * ZTOK:(zz + 1) * ZTOK].reshape(ZCOLS, ZTOK), NT)
        acc = term if acc is None else acc + term
    grad[...] = acc.reshape(LINE, RBLOCKS, ZCOLS)
    squares = jnp.zeros((8, 128), F32)
    for zz in range(LINE):
        piece = grad[zz]
        high, low = parts(piece)
        wg[zz, :, 0:RBLOCKS] = dot_across(high) + dot(across[0:64], low, NT)
        sq = piece * piece
        for lane in range(4):
            squares += jnp.sum(sq[:, lane * 128:(lane + 1) * 128].reshape(10, 8, 128), axis=0)
    regroup_w(wg, pg_send)
    for q in range(PLANE):
        pg_send[q, 16:24, :] = squares
    pg_copies = plane_start(pg_send, pg_recv, spg, rpg)
    for d in range(1, 4):
        to = shift(z, d)
        grad_copies.append(go(copy(grad.at[to], grad_row.at[z], sgr.at[d - 1], rgr.at[d - 1], core, to, me)))
    grad_row[z] = grad[z]
    for step in MSTEPS[0]:
        momentum_step(step)
    for c in pg_copies:
        wait(c)
    v_copies = {}
    high, low = parts(pg_recv[:, 0:16, :].reshape(256, 128))
    both = dot(keep[...], high, NN)
    coef[core, 0:32, :] = both[0:32] + both[32:64] + dot(keep[0:32], low, NN)
    plane_sq = jnp.sum(pg_recv[:, 16:24, :], axis=0)
    plane_sq = jnp.sum(jnp.sum(plane_sq, axis=0, keepdims=True), axis=1, keepdims=True)
    coef[core, 32:40, :] = jnp.broadcast_to(plane_sq, (8, 128))
    share = go(copy(coef.at[core], coef.at[core], sfg.at[0], rfg.at[0], 1 - core, z, me))
    wait(share)
    high, low = parts(jnp.concatenate([coef[0, 0:32], coef[1, 0:32]], axis=0))
    result = dot(back[...], jnp.concatenate([high, low, high], axis=0), NN)
    row = lax.broadcasted_iota(jnp.int32, (8, 128), 0)
    lane = lax.broadcasted_iota(jnp.int32, (8, 128), 1)
    sums = jnp.where(row < 4, coef[0, 32:40], coef[1, 32:40])
    vg[...] = result.reshape(64, 8, 128) + jnp.where(lane >= RBLOCKS, sums, F32(0.0))[None]
    for dz, d in sorted(((dz, d) for dz in range(4) for d in range(16)), key=lambda v: -hops(*v)):
        if dz or d:
            zz, ii = shift(z, dz), inplane(d)
            v_copies[dz, d] = go(copy(
                vg.at[zz * 16 + ii], vg_all.at[t], sqg.at[dz, d], rqg.at[dz, d], core, zz, ii))
    vg_all[t] = vg[t]
    for step in MSTEPS[1]:
        momentum_step(step)
    for c in v_copies.values():
        wait(c)

    factors = []
    for r in range(2):
        square = vg_all[0, 4 * r:4 * r + 1, 127:128]
        for zz in range(1, LINE):
            square = square + vg_all[zz * 16, 4 * r:4 * r + 1, 127:128]
        factors.append(jnp.minimum(F32(1.0), 1.0 / jnp.sqrt(square / (RBLOCKS * BLOCK * COLS) + 1e-06)))
    factor = jnp.where(core == 0, factors[0], factors[1])
    row = lax.broadcasted_iota(jnp.int32, (8, 128), 0)
    by_row = jnp.where(row < 4, factors[0], factors[1])
    total_v[...] = (F32(0.9) * vm_rows[...] + by_row[None] * vg_all[...]).reshape(512, 128)
    for c in grad_copies:
        wait(c)
    for g in range(8):
        cols = slice(g * 256, (g + 1) * 256)
        local = slice((g % 2) * 256, (g % 2) * 256 + 256)
        high, low = parts(total_v[g * 64:(g + 1) * 64, :])
        kept = dot(jnp.concatenate([high, low, high], axis=0), spread[core], TN)[0:RBLOCKS]
        full = F32(0.9) * mom[:, cols].astype(F32) + factor * grad_row[g // 2, :, local]
        new_out[:, cols] = (full - kept[:, 0:256]).astype(BF16)
        upd_out[:, cols] = kept[:, 256:512].astype(BF16)
    for c in sent:
        if id(c) not in arrived:
            c.wait_recv()
        c.wait_send()


def body(activations, head_grads, momentum):
    dma = pltpu.SemaphoreType.DMA
    consts = [jnp.asarray(c) for c in tables()]
    vmem = pl.BlockSpec(memory_space=pltpu.VMEM)
    hbm = pl.BlockSpec(memory_space=pltpu.HBM)
    scratch = [
        pltpu.VMEM((32, RBLOCKS * BLOCK), BF16),
        pltpu.VMEM((RBLOCKS, COLS), BF16),
    ] + [pltpu.VMEM(c.shape, BF16) for c in consts] + [
        pltpu.VMEM((640, 256), BF16),
        pltpu.VMEM((PLANE, 32, 384), BF16),
        pltpu.VMEM((PLANE, 32, 384), BF16),
        pltpu.VMEM((LINE, 4, 320, 128), BF16),
        pltpu.VMEM((PLANE, 32, TOKENS), BF16),
        pltpu.VMEM((LINE, RBLOCKS, ZCOLS), F32),
        pltpu.VMEM((LINE, RBLOCKS, ZCOLS), F32),
        pltpu.VMEM((LINE, 64, 128), F32),
        pltpu.VMEM((LINE, 64, 128), F32),
        pltpu.VMEM((PLANE, 16, 128), F32),
        pltpu.VMEM((PLANE, 16, 128), F32),
        pltpu.VMEM((PLANE, 16, 128), F32),
        pltpu.VMEM((PLANE, 16, 128), F32),
        pltpu.VMEM((LINE, 64, 128), F32),
        pltpu.VMEM((2, LINE, 64, 128), F32),
        pltpu.VMEM((LINE, 64, 128), F32),
        pltpu.VMEM((PLANE, 24, 128), F32),
        pltpu.VMEM((PLANE, 24, 128), F32),
        pltpu.VMEM((2, 40, 128), F32),
        pltpu.VMEM((64, 8, 128), F32),
        pltpu.VMEM((64, 8, 128), F32),
        pltpu.VMEM((64, 8, 128), F32),
        pltpu.VMEM((512, 128), F32),
        dma((10,)),
    ]
    for shape in ((15,), (4, 4), (2, 20), (3,), (3,), (15,), (15,), (2, 4), (15,), (4, 16), (1,)):
        scratch += [dma(shape), dma(shape)]
    new, upd = pl.pallas_call(
        kernel,
        out_shape=(
            pltpu.VMEM((RBLOCKS, COLS), BF16),
            pltpu.VMEM((RBLOCKS, COLS), BF16),
        ),
        in_specs=[hbm] * 10,
        out_specs=(vmem, vmem),
        scratch_shapes=scratch,
        compiler_params=pltpu.CompilerParams(
            collective_id=0, has_side_effects=True, vmem_limit_bytes=48 * 1024 * 1024
        ),
    )(*(pltpu.with_memory_space_constraint(v, pltpu.HBM)
        for v in (activations, head_grads.T, momentum.reshape(RBLOCKS, COLS), *consts)))

    def store(new_ref, upd_ref, new_hbm, upd_hbm, sems):
        copies = (
            pltpu.make_async_copy(new_ref, new_hbm, sems.at[0]),
            pltpu.make_async_copy(upd_ref, upd_hbm, sems.at[1]),
        )
        for c in copies:
            c.start()
        for c in copies:
            c.wait()

    new, upd = pl.pallas_call(
        store,
        out_shape=(
            jax.ShapeDtypeStruct((RBLOCKS, COLS), BF16),
            jax.ShapeDtypeStruct((RBLOCKS, COLS), BF16),
        ),
        in_specs=[vmem] * 2,
        out_specs=(hbm, hbm),
        scratch_shapes=[dma((2,))],
    )(*(pltpu.with_memory_space_constraint(v, pltpu.VMEM) for v in (new, upd)))
    return new[None, None], upd[None]


def solution(mesh):
    placed = (P(("dp", "tensor"), None), P("dp", "tensor"), P("dp", "tensor", None, None))
    return jax.shard_map(
        body,
        mesh=mesh,
        in_specs=placed,
        out_specs=(P("dp", "tensor", None, None), P("tensor", None, None)),
        check_vma=False,
    )
```

time: 64.6 us -> 50.5 us (0.78)
  local copies, waits for them, and re-layouts: 7.89 us -> 0 us
  Pallas kernels: 55.7 us -> 49.7 us
    unnamed x19 -> x0, local copies, waits for them, and re-layouts: 7.89 us -> none
    pallas_call x1 -> x2, Pallas kernels: 55.7 us -> 49.7 us  [the longest x1 48.8 us: body(): pl.pallas_call(kernel, out_shape=(pltpu.VMEM((RBLOCKS, COLS), BF16), pltp...]
where the time goes in v2:
time: 50.5 us; the launch traced here: 50.3 us
  Pallas kernels  49.7 us (98%)
  between operations  0.64 us (1%)
    pallas_call x1, Pallas kernels, body(): pl.pallas_call(kernel, out_shape=(pltpu.VMEM((RBLOCKS, COLS), BF16), pltp...  48.8 us

profile of v2, /device:TPU:1, one launch (start us, length us, event | category | flops | bytes accessed | tf_op | source)
XLA Modules:
  0.0 50.3 jit_solution(7894636094225736028)
XLA Ops:
  0.6 48.8 %shard_map.113 = (bf16[80,2048]{1,0:T(8,128)(2,1)S(1)}, bf16[80,2048]{1,0:T(8,128)(2,1)S(1)}) custom-call(bf16[32,5120]{1,0:T(8,128)(2,1)} %act_hbm.1, bf16[32,2048]{1,0:T(8,128)(2,1)} %bitcast.5, bf16[80,2048]{1,0:T(8,128)(2,1)} %bitcast.4, bf16[256,256]{1,0:T(8,128)(2,1)} %constant.14.clone.sort_hbm, bf16[320,384]{1,0:T(8,128)(2,1)} %constant.15.clone.pick_hbm, ...), custom_call_target="tpu_custom_call" | custom-call | tf_op jit(solution)/shard_map/pallas_call | solution.py:494
  49.5 0.9 %shard_map.114 = (bf16[80,2048]{1,0:T(8,128)(2,1)}, bf16[80,2048]{1,0:T(8,128)(2,1)}) custom-call(bf16[80,2048]{1,0:T(8,128)(2,1)S(1)} %get-tuple-element.6.new_ref, bf16[80,2048]{1,0:T(8,128)(2,1)S(1)} %get-tuple-element.7.upd_ref), custom_call_target="tpu_custom_call" | custom-call | tf_op jit(solution)/shard_map/pallas_call | solution.py:519

commit v3 on v2

--- a/solution.py
+++ b/solution.py
@@ -18,15 +18,17 @@
 PLANE = 16
 ZCOLS = COLS // LINE
 ZTOK = TOKENS // LINE
+OWN = 5
+ROWS = 400
 MESH = pl.DeviceIdType.MESH
 F32 = jnp.float32
 BF16 = jnp.bfloat16
 NT = (((1,), (1,)), ((), ()))
 TN = (((0,), (0,)), ((), ()))
 NN = (((1,), (0,)), ((), ()))
-ORDER = ("a0", "a1", "a3", "s", "a2", "g0", "z0", "f", "z1", "z3", "g1", "g2", "z2", "g3", "m1")
+ORDER = ("a0", "a1", "a3", "s", "a2", "m1", "g0", "z0", "f", "z1", "m2", "z3", "g1", "g2", "z2", "g3", "m3")
 START = "A12"
-MSTEPS = ((2,), (3, 4))
+MSTEPS = (4,)
 AORD = (1, 3, 2, 4, 12, 5, 7, 13, 15, 6, 14, 8, 9, 11, 10)
 
 
@@ -46,35 +48,47 @@
         for z in range(LINE):
             for i in range(PLANE):
                 sort[a * 64 + z * 16 + i, i * 16 + z * 4 + a] = 1
-    pick = np.zeros((LINE * RBLOCKS, 384))
+    pick = np.zeros((ROWS, 640))
     for tile in range(RBLOCKS // 4):
         for z in range(LINE):
             for a in range(4):
-                pick[z * RBLOCKS + 4 * tile + a, tile * 16 + z * 4 + a] = 1
+                lane = tile * 16 + z * 4 + a
+                pick[z * RBLOCKS + 4 * tile + a, lane] = 1
+                if tile >= 16:
+                    pick[z * RBLOCKS + 4 * tile + a, lane + 192] = 1
+    for k in range(OWN * KEEP):
+        pick[320 + k, 512 + k] = 1
+        pick[360 + k, 576 + k] = 1
+    squeeze = np.zeros((2, 384, 128))
+    for odd in range(2):
+        for part, table in enumerate(split(basis)):
+            for j in range(OWN):
+                top = (j + odd) * BLOCK
+                squeeze[odd, top:top + BLOCK, part * 64 + j * KEEP:part * 64 + (j + 1) * KEEP] = table.T.astype(np.float64)
     across = np.kron(np.eye(8), basis)
+    across_h, across_l = split(across)
+    twice = np.stack([np.concatenate([v, v], axis=0) for v in (across_h, across_l)])
+    expand = np.concatenate([across_h, across_h, across_l], axis=0)
     order = np.array([z * PLANE + i for i in range(PLANE) for z in range(LINE)])
     project = np.kron((basis.T @ basis)[np.ix_(order, order)], np.eye(4))
-    gather_n = np.kron(basis[:, order], np.eye(4))
-    back = np.zeros((BLOCK, 2, 4, 2, KEEP, 4))
-    spread = np.zeros((2, 4, 2, 2, 4, 2, 4, BLOCK))
+    back = np.zeros((BLOCK, 8, 48))
+    for j in range(OWN):
+        back[:, j, j * KEEP:(j + 1) * KEEP] = basis.T
+    back_h, back_l = split(back.reshape(512, 48))
+    back = np.concatenate([back_h, back_h, back_l], axis=1)
+    spread = np.zeros((2, 2, 64, 2, 512))
     for r in range(2):
-        for l in range(4):
-            back[:, r, l, r, :, l] = basis.T
-        for b in range(4):
-            for half in range(2):
-                rows = basis[half * 4:half * 4 + 4]
-                spread[r, b, half, r, :, 0, b] = rows
-                spread[:, b, half, r, :, 1, b] = 0.5 * rows
-    back_h, back_l = split(back.reshape(512, 64))
-    back = np.concatenate([back_h, back_h, back_l], axis=1)
-    spread_h, spread_l = split(spread.reshape(2, 64, 512))
+        spread[r, r, :, 0] = across
+        spread[r, :, :, 1] = 0.5 * across
+    spread_h, spread_l = split(spread.reshape(2, 128, 1024))
     spread = np.concatenate([spread_h, spread_h, spread_l], axis=1)
     return (
         sort.astype(ml_dtypes.bfloat16),
         pick.astype(ml_dtypes.bfloat16),
-        np.concatenate(split(across), axis=0),
+        squeeze.astype(ml_dtypes.bfloat16),
+        twice,
+        expand,
         np.stack(split(project)),
-        np.concatenate(split(gather_n), axis=0),
         back,
         spread,
     )
@@ -90,14 +104,14 @@
 
 
 def kernel(
-    act_hbm, head_hbm, mom_hbm, sort_hbm, pick_hbm, across_hbm, project_hbm, keep_hbm, back_hbm, spread_hbm,
+    act_hbm, head_hbm, mom_hbm, sort_hbm, pick_hbm, squeeze_hbm, twice_hbm, expand_hbm, project_hbm, back_hbm, spread_hbm,
     new_out, upd_out,
-    act, mom, sort, pick, across, project, keep, back, spread, stack,
-    a_send, a_recv, at, gt, grad, grad_row,
+    act, mom, sort, pick, squeeze, twice, expand, project, back, spread, stack, windows,
+    a_send, a_recv, tokens, at, gt, grad, grad_row,
     wm_send, wm_recv, pm_send, pm_recv, qm_send, qm_recv, vm, vm_all,
-    wg, pg_send, pg_recv, coef, vg, vg_all, vm_rows, total_v,
+    coef, vg, vg_all, packed, base_new, base_upd,
     load, sa, ra, sz, rz, sg, rg, sgr, rgr, swm, rwm,
-    spm, rpm, sqm, rqm, svm, rvm, spg, rpg, sqg, rqg, sfg, rfg,
+    spm, rpm, sqm, rqm, svm, rvm, sqg, rqg, sfg, rfg,
 ):
     core = lax.axis_index("dp")
     t = lax.axis_index("tensor")
@@ -141,9 +155,9 @@
 
     loads = {}
     for k, (name, src, dst) in enumerate((
-        ("act", act_hbm, act), ("sort", sort_hbm, sort), ("head", head_hbm, gt.at[me]),
-        ("mom", mom_hbm, mom), ("pick", pick_hbm, pick), ("across", across_hbm, across),
-        ("project", project_hbm, project), ("keep", keep_hbm, keep), ("back", back_hbm, back), ("spread", spread_hbm, spread),
+        ("act", act_hbm, act), ("sort", sort_hbm, sort), ("squeeze", squeeze_hbm, squeeze), ("head", head_hbm, gt.at[me]),
+        ("mom", mom_hbm, mom), ("pick", pick_hbm, pick), ("twice", twice_hbm, twice), ("expand", expand_hbm, expand),
+        ("project", project_hbm, project), ("back", back_hbm, back), ("spread", spread_hbm.at[core], spread),
     )):
         loads[name] = pltpu.make_async_copy(src, dst, load.at[k])
         loads[name].start()
@@ -171,9 +185,46 @@
                         v[k] = jnp.where(low, a, pltpu.roll(b, 16 * d, 1))
                         v[k | d] = jnp.where(low, pltpu.roll(a, 128 - 16 * d, 1), b)
             for k in range(8):
-                a_send[half * 8 + k, :, octet * 128:(octet + 1) * 128] = v[k].astype(BF16)
-
+                upper_rows, lower_rows = v[k][0:16], v[k][16:32]
+                if octet < 2:
+                    a_send[half * 8 + k, :, octet * 128:octet * 128 + 128] = upper_rows.astype(BF16)
+                    a_send[half * 8 + k, :, octet * 128 + 256:octet * 128 + 384] = lower_rows.astype(BF16)
+                else:
+                    folded = jnp.where(group[0:16] < 4, upper_rows, pltpu.roll(lower_rows, 64, 1))
+                    a_send[half * 8 + k, :, 512:640] = folded.astype(BF16)
+
+    loads["squeeze"].wait()
+    first_half = lax.broadcasted_iota(jnp.int32, (256, 128), 1) < 64
+    for odd in range(2):
+        for m in range(8):
+            windows[odd, m * 32:(m + 1) * 32, :] = act[:, m * 640 + odd * 256:m * 640 + odd * 256 + 384]
+        both = dot(windows[odd], squeeze[odd], NN)
+        both = both + pltpu.roll(both, 64, 1)
+        high = both.astype(BF16).astype(F32)
+        both = jnp.where(first_half, high, both - high).astype(BF16)
+        for m in range(8):
+            a_send[2 * m + odd, :, 640:768] = both[m * 32:m * 32 + 16]
+            a_send[2 * m + odd, :, 768:896] = both[m * 32 + 16:m * 32 + 32]
+
+    for name in ("mom", "twice"):
+        loads[name].wait()
+    wm_send[...] = jnp.zeros_like(wm_send)
+    coef[core] = jnp.zeros((56, 128), F32)
+    for zz in range(LINE):
+        piece = mom[:, zz * ZCOLS:(zz + 1) * ZCOLS]
+        wm_send[zz, :, 0:RBLOCKS] = dot(twice[0, 0:64], piece, NT) + dot(twice[1, 0:64], piece, NT)
     pl.semaphore_wait(barrier, len(partners))
+
+    wm_copies = []
+
+    def wm_start():
+        for d in range(1, 4):
+            to = shift(z, d)
+            wm_copies.append(go(copy(wm_send.at[to], wm_recv.at[z], swm.at[d - 1], rwm.at[d - 1], core, to, me)))
+        wm_recv[z] = wm_send[z]
+
+    wm_start()
+
 
     loads["head"].wait()
 
@@ -212,33 +263,16 @@
 
 
     a_recv[me] = a_send[me]
+    tokens[...] = jnp.zeros_like(tokens)
     for step in START:
         {"A": lambda: start_a(AORD), "1": start_g1, "2": start_g2}[step]()
 
-    def dot_across(piece):
-        both = dot(across[...], piece, NT)
-        return both[0:64] + both[64:128]
-
-    for name in ("mom", "across", "pick", "project", "keep", "back", "spread"):
+    for name in ("pick", "expand", "project", "back", "spread"):
         loads[name].wait()
-    wm_send[...] = jnp.zeros_like(wm_send)
-    wg[...] = jnp.zeros_like(wg)
-    for zz in range(LINE):
-        piece = mom[:, zz * ZCOLS:(zz + 1) * ZCOLS]
-        wm_send[zz, :, 0:RBLOCKS] = dot_across(piece)
-    wm_copies = []
-
-    def wm_start():
-        for d in range(1, 4):
-            to = shift(z, d)
-            wm_copies.append(go(copy(wm_send.at[to], wm_recv.at[z], swm.at[d - 1], rwm.at[d - 1], core, to, me)))
-        wm_recv[z] = wm_send[z]
-
-    wm_start()
 
     z_copies = {}
     zu, zd, zo = shift(z, 1), shift(z, -1), shift(z, 2)
-    every, first, second = (0, 320), (0, 160), (160, 160)
+    every, first, second = (0, 400), (0, 208), (208, 192)
 
     def z_go(slot, dy, rows, sem, to):
         where = at.at[slot, shift(y, dy), pl.ds(rows[0], rows[1]), :]
@@ -253,8 +287,16 @@
             if d:
                 wait(a_copies[d])
         line = shift(y, dy)
-        tokens = a_recv[pl.ds(line * 4, 4)].reshape(128, 384)
-        at[z, line] = dot(pick[...], tokens, NT).astype(BF16)
+        for src in range(4):
+            here = a_recv.at[line * 4 + src]
+            top, low = slice(src * 32, src * 32 + 16), slice(src * 32 + 16, src * 32 + 32)
+            tokens[top, 0:256] = here[:, 0:256]
+            tokens[top, 256:384] = here[:, 512:640]
+            tokens[low, 0:256] = here[:, 256:512]
+            tokens[low, 384:512] = here[:, 512:640]
+            tokens[top, 512:640] = here[:, 640:768]
+            tokens[low, 512:640] = here[:, 768:896]
+        at[z, line] = dot(pick[...], tokens[...], NT).astype(BF16)
         z_go(z, dy, every, 0, zu)
         z_go(z, dy, every, 1, zd)
 
@@ -330,10 +372,15 @@
         else:
             for c in line_end(vm_copies[0], vm_all, svm, rvm):
                 wait(c)
-            for r in range(2):
-                for zz in range(LINE):
-                    for q in range(PLANE):
-                        vm_rows[zz * 16 + q, 4 * r:4 * r + 4, :] = vm_all[r, zz, 4 * q:4 * q + 4, :]
+            for zz in range(LINE):
+                cols = slice(zz * ZCOLS, (zz + 1) * ZCOLS)
+                pair = []
+                for r in range(2):
+                    high, low = parts(vm_all[r, zz])
+                    pair.append(dot(jnp.concatenate([high, low, high], axis=0), expand[...], TN)[0:RBLOCKS])
+                base_upd[:, cols] = F32(0.45) * (pair[0] + pair[1])
+                own = jnp.where(core == 0, pair[0], pair[1])
+                base_new[:, cols] = F32(0.9) * (mom[:, cols].astype(F32) - own)
 
     def near_chunks():
         for half in range(2):
@@ -372,83 +419,64 @@
         for half in range(2):
             g_wait(half, 6 + 4 * j)
             g_wait(half, 7 + 4 * j)
+    grad_copies = []
+
+    def term(zz):
+        left = jnp.concatenate([at[zz, yy] for yy in range(4)], axis=1)
+        right = gt[:, :, pl.ds(pl.multiple_of(zz * ZTOK, ZTOK), ZTOK)]
+        return dot(left, right.reshape(ZCOLS, ZTOK), NT)
+
+    acc = term(z) + term(zd) + term(zu)
     for dy in (0, 1, 3, 2):
         z_wait(dy, 2)
         z_wait(dy, 3)
-
-    grad_copies, pg_copies, qg_copies, vg_copies = [], [], [], []
-    acc = None
-    for zz in range(LINE):
-        left = jnp.concatenate([at[zz, yy] for yy in range(4)], axis=1)
-        term = dot(left, gt[:, :, zz * ZTOK:(zz + 1) * ZTOK].reshape(ZCOLS, ZTOK), NT)
-        acc = term if acc is None else acc + term
-    grad[...] = acc.reshape(LINE, RBLOCKS, ZCOLS)
-    squares = jnp.zeros((8, 128), F32)
-    for zz in range(LINE):
-        piece = grad[zz]
-        high, low = parts(piece)
-        wg[zz, :, 0:RBLOCKS] = dot_across(high) + dot(across[0:64], low, NT)
-        sq = piece * piece
-        for lane in range(4):
-            squares += jnp.sum(sq[:, lane * 128:(lane + 1) * 128].reshape(10, 8, 128), axis=0)
-    regroup_w(wg, pg_send)
-    for q in range(PLANE):
-        pg_send[q, 16:24, :] = squares
-    pg_copies = plane_start(pg_send, pg_recv, spg, rpg)
+    acc = acc + term(zo)
+    rows = acc[0:320]
+    grad[...] = rows.reshape(LINE, RBLOCKS, ZCOLS)
+    square = jnp.sum(jnp.sum(rows * rows, axis=0, keepdims=True), axis=1, keepdims=True)
     for d in range(1, 4):
         to = shift(z, d)
         grad_copies.append(go(copy(grad.at[to], grad_row.at[z], sgr.at[d - 1], rgr.at[d - 1], core, to, me)))
     grad_row[z] = grad[z]
-    for step in MSTEPS[0]:
-        momentum_step(step)
-    for c in pg_copies:
-        wait(c)
+    mine = lax.broadcasted_iota(jnp.int32, (40, 128), 1) // 64 == core
+    high, low = parts(acc[320:360] + acc[360:400])
+    own = dot(high, twice[0], NT) + dot(low, twice[0], NT) + dot(high, twice[1], NT)
+    coef[core, 0:40, :] = jnp.where(mine, own, F32(0.0))
+    coef[core, 48:56, :] = jnp.where(mine[0:8], jnp.broadcast_to(square, (8, 128)), F32(0.0))
+    share = go(copy(coef.at[core], coef.at[core], sfg.at[0], rfg.at[0], 1 - core, z, me))
     v_copies = {}
-    high, low = parts(pg_recv[:, 0:16, :].reshape(256, 128))
-    both = dot(keep[...], high, NN)
-    coef[core, 0:32, :] = both[0:32] + both[32:64] + dot(keep[0:32], low, NN)
-    plane_sq = jnp.sum(pg_recv[:, 16:24, :], axis=0)
-    plane_sq = jnp.sum(jnp.sum(plane_sq, axis=0, keepdims=True), axis=1, keepdims=True)
-    coef[core, 32:40, :] = jnp.broadcast_to(plane_sq, (8, 128))
-    share = go(copy(coef.at[core], coef.at[core], sfg.at[0], rfg.at[0], 1 - core, z, me))
     wait(share)
-    high, low = parts(jnp.concatenate([coef[0, 0:32], coef[1, 0:32]], axis=0))
+    high, low = parts(coef[0, 0:48] + coef[1, 0:48])
     result = dot(back[...], jnp.concatenate([high, low, high], axis=0), NN)
+    sums = coef[0, 48:56] + coef[1, 48:56]
     row = lax.broadcasted_iota(jnp.int32, (8, 128), 0)
-    lane = lax.broadcasted_iota(jnp.int32, (8, 128), 1)
-    sums = jnp.where(row < 4, coef[0, 32:40], coef[1, 32:40])
-    vg[...] = result.reshape(64, 8, 128) + jnp.where(lane >= RBLOCKS, sums, F32(0.0))[None]
+    vg[...] = result.reshape(64, 8, 128) + jnp.where(row == 5, sums, F32(0.0))[None]
     for dz, d in sorted(((dz, d) for dz in range(4) for d in range(16)), key=lambda v: -hops(*v)):
         if dz or d:
             zz, ii = shift(z, dz), inplane(d)
             v_copies[dz, d] = go(copy(
                 vg.at[zz * 16 + ii], vg_all.at[t], sqg.at[dz, d], rqg.at[dz, d], core, zz, ii))
     vg_all[t] = vg[t]
-    for step in MSTEPS[1]:
+    for step in MSTEPS:
         momentum_step(step)
     for c in v_copies.values():
         wait(c)
 
-    factors = []
-    for r in range(2):
-        square = vg_all[0, 4 * r:4 * r + 1, 127:128]
-        for zz in range(1, LINE):
-            square = square + vg_all[zz * 16, 4 * r:4 * r + 1, 127:128]
-        factors.append(jnp.minimum(F32(1.0), 1.0 / jnp.sqrt(square / (RBLOCKS * BLOCK * COLS) + 1e-06)))
-    factor = jnp.where(core == 0, factors[0], factors[1])
-    row = lax.broadcasted_iota(jnp.int32, (8, 128), 0)
-    by_row = jnp.where(row < 4, factors[0], factors[1])
-    total_v[...] = (F32(0.9) * vm_rows[...] + by_row[None] * vg_all[...]).reshape(512, 128)
+    square = jnp.sum(vg_all[:, 5:6, :], axis=0)
+    factors = jnp.minimum(F32(1.0), 1.0 / jnp.sqrt(square / (RBLOCKS * BLOCK * COLS) + 1e-06))
+    factor = jnp.where(core == 0, factors[:, 0:1], factors[:, 127:128])
+    for zz in range(LINE):
+        for i in range(PLANE):
+            packed[zz * RBLOCKS + OWN * i:zz * RBLOCKS + OWN * (i + 1), :] = vg_all[zz * 16 + i, 0:OWN, :]
+    high, low = parts(packed[...] * factors)
+    kept = dot(jnp.concatenate([high, low, high], axis=1), spread[...], NN)
     for c in grad_copies:
         wait(c)
-    for g in range(8):
-        cols = slice(g * 256, (g + 1) * 256)
-        local = slice((g % 2) * 256, (g % 2) * 256 + 256)
-        high, low = parts(total_v[g * 64:(g + 1) * 64, :])
-        kept = dot(jnp.concatenate([high, low, high], axis=0), spread[core], TN)[0:RBLOCKS]
-        full = F32(0.9) * mom[:, cols].astype(F32) + factor * grad_row[g // 2, :, local]
-        new_out[:, cols] = (full - kept[:, 0:256]).astype(BF16)
-        upd_out[:, cols] = kept[:, 256:512].astype(BF16)
+    for zz in range(LINE):
+        cols = slice(zz * ZCOLS, (zz + 1) * ZCOLS)
+        rows = slice(zz * RBLOCKS, (zz + 1) * RBLOCKS)
+        new_out[:, cols] = (base_new[:, cols] + (factor * grad_row[zz] - kept[rows, 0:512])).astype(BF16)
+        upd_out[:, cols] = (base_upd[:, cols] + kept[rows, 512:1024]).astype(BF16)
     for c in sent:
         if id(c) not in arrived:
             c.wait_recv()
@@ -463,11 +491,13 @@
     scratch = [
         pltpu.VMEM((32, RBLOCKS * BLOCK), BF16),
         pltpu.VMEM((RBLOCKS, COLS), BF16),
-    ] + [pltpu.VMEM(c.shape, BF16) for c in consts] + [
+    ] + [pltpu.VMEM(c.shape, BF16) for c in consts[:-1]] + [pltpu.VMEM(consts[-1].shape[1:], BF16)] + [
         pltpu.VMEM((640, 256), BF16),
-        pltpu.VMEM((PLANE, 32, 384), BF16),
-        pltpu.VMEM((PLANE, 32, 384), BF16),
-        pltpu.VMEM((LINE, 4, 320, 128), BF16),
+        pltpu.VMEM((2, 256, 384), BF16),
+        pltpu.VMEM((PLANE, 16, 896), BF16),
+        pltpu.VMEM((PLANE, 16, 896), BF16),
+        pltpu.VMEM((128, 640), BF16),
+        pltpu.VMEM((LINE, 4, ROWS, 128), BF16),
         pltpu.VMEM((PLANE, 32, TOKENS), BF16),
         pltpu.VMEM((LINE, RBLOCKS, ZCOLS), F32),
         pltpu.VMEM((LINE, RBLOCKS, ZCOLS), F32),
@@ -479,17 +509,15 @@
         pltpu.VMEM((PLANE, 16, 128), F32),
         pltpu.VMEM((LINE, 64, 128), F32),
         pltpu.VMEM((2, LINE, 64, 128), F32),
-        pltpu.VMEM((LINE, 64, 128), F32),
-        pltpu.VMEM((PLANE, 24, 128), F32),
-        pltpu.VMEM((PLANE, 24, 128), F32),
-        pltpu.VMEM((2, 40, 128), F32),
+        pltpu.VMEM((2, 56, 128), F32),
         pltpu.VMEM((64, 8, 128), F32),
         pltpu.VMEM((64, 8, 128), F32),
-        pltpu.VMEM((64, 8, 128), F32),
-        pltpu.VMEM((512, 128), F32),
-        dma((10,)),
+        pltpu.VMEM((LINE * RBLOCKS, 128), F32),
+        pltpu.VMEM((RBLOCKS, COLS), F32),
+        pltpu.VMEM((RBLOCKS, COLS), F32),
+        dma((11,)),
     ]
-    for shape in ((15,), (4, 4), (2, 20), (3,), (3,), (15,), (15,), (2, 4), (15,), (4, 16), (1,)):
+    for shape in ((15,), (4, 4), (2, 20), (3,), (3,), (15,), (15,), (2, 4), (4, 16), (1,)):
         scratch += [dma(shape), dma(shape)]
     new, upd = pl.pallas_call(
         kernel,
@@ -497,7 +525,7 @@
             pltpu.VMEM((RBLOCKS, COLS), BF16),
             pltpu.VMEM((RBLOCKS, COLS), BF16),
         ),
-        in_specs=[hbm] * 10,
+        in_specs=[hbm] * 11,
         out_specs=(vmem, vmem),
         scratch_shapes=scratch,
         compiler_params=pltpu.CompilerParams(

time: 50.5 us -> 47.2 us (0.935)
  Pallas kernels: 49.7 us -> 46.3 us
    pallas_call x1, Pallas kernels: 48.8 us -> 45.4 us  [body(): pl.pallas_call(kernel, out_shape=(pltpu.VMEM((RBLOCKS, COLS), BF16), pltp...]
where the time goes in v3:
time: 47.2 us; the launch traced here: 46.9 us
  Pallas kernels  46.3 us (98%)
  between operations  0.64 us (1%)
    pallas_call x1, Pallas kernels, body(): pl.pallas_call(kernel, out_shape=(pltpu.VMEM((RBLOCKS, COLS), BF16), pltp...  45.4 us

profile of v3, /device:TPU:1, one launch (start us, length us, event | category | flops | bytes accessed | tf_op | source)
XLA Modules:
  0.0 46.9 jit_solution(14044465705657813242)
XLA Ops:
  0.6 45.4 %shard_map.122 = (bf16[80,2048]{1,0:T(8,128)(2,1)S(1)}, bf16[80,2048]{1,0:T(8,128)(2,1)S(1)}) custom-call(bf16[32,5120]{1,0:T(8,128)(2,1)} %act_hbm.1, bf16[32,2048]{1,0:T(8,128)(2,1)} %bitcast.5, bf16[80,2048]{1,0:T(8,128)(2,1)} %bitcast.4, bf16[256,256]{1,0:T(8,128)(2,1)} %constant.16.clone.sort_hbm, bf16[400,640]{1,0:T(8,128)(2,1)} %constant.17.clone.pick_hbm, ...), custom_call_target="tpu_custom_call" | custom-call | tf_op jit(solution)/shard_map/pallas_call | solution.py:522
  46.1 0.9 %shard_map.123 = (bf16[80,2048]{1,0:T(8,128)(2,1)}, bf16[80,2048]{1,0:T(8,128)(2,1)}) custom-call(bf16[80,2048]{1,0:T(8,128)(2,1)S(1)} %get-tuple-element.6.new_ref, bf16[80,2048]{1,0:T(8,128)(2,1)S(1)} %get-tuple-element.7.upd_ref), custom_call_target="tpu_custom_call" | custom-call | tf_op jit(solution)/shard_map/pallas_call | solution.py:547

commit v4 on v3

--- a/solution.py
+++ b/solution.py
@@ -19,6 +19,7 @@
 ZCOLS = COLS // LINE
 ZTOK = TOKENS // LINE
 OWN = 5
+SHARE = 1024
 ROWS = 400
 MESH = pl.DeviceIdType.MESH
 F32 = jnp.float32
@@ -26,8 +27,8 @@
 NT = (((1,), (1,)), ((), ()))
 TN = (((0,), (0,)), ((), ()))
 NN = (((1,), (0,)), ((), ()))
-ORDER = ("a0", "a1", "a3", "s", "a2", "m1", "g0", "z0", "f", "z1", "m2", "z3", "g1", "g2", "z2", "g3", "m3")
-START = "A12"
+ORDER = ("a0", "s", "a1", "a3", "a2", "m1", "f", "g0", "z0", "g1", "g2", "z1", "m2", "g3", "z3", "z2", "m3")
+START = "1A2"
 MSTEPS = (4,)
 AORD = (1, 3, 2, 4, 12, 5, 7, 13, 15, 6, 14, 8, 9, 11, 10)
 
@@ -36,6 +37,10 @@
     high = table.astype(np.float32).astype(ml_dtypes.bfloat16)
     low = (table - high.astype(np.float64)).astype(np.float32).astype(ml_dtypes.bfloat16)
     return high, low
+
+
+def device(core, line, place):
+    return line * 16 + place + core * (place // 4 * 16 + line * 4 + place % 4 - line * 16 - place)
 
 
 def tables():
@@ -43,11 +48,12 @@
     n = np.arange(BLOCK)[None, :]
     scale = np.where(k == 0, math.sqrt(1.0 / BLOCK), math.sqrt(2.0 / BLOCK))
     basis = scale * np.cos(math.pi * (2 * n + 1) * k / (2 * BLOCK))
-    sort = np.zeros((256, 256))
+    sort = np.zeros((2, 256, 256))
     for a in range(4):
         for z in range(LINE):
             for i in range(PLANE):
-                sort[a * 64 + z * 16 + i, i * 16 + z * 4 + a] = 1
+                for core in range(2):
+                    sort[core, a * 64 + device(core, z, i), i * 16 + z * 4 + a] = 1
     pick = np.zeros((ROWS, 640))
     for tile in range(RBLOCKS // 4):
         for z in range(LINE):
@@ -69,18 +75,19 @@
     across_h, across_l = split(across)
     twice = np.stack([np.concatenate([v, v], axis=0) for v in (across_h, across_l)])
     expand = np.concatenate([across_h, across_h, across_l], axis=0)
-    order = np.array([z * PLANE + i for i in range(PLANE) for z in range(LINE)])
-    project = np.kron((basis.T @ basis)[np.ix_(order, order)], np.eye(4))
+    project = []
+    for core in range(2):
+        order = np.array([device(core, z, i) for i in range(PLANE) for z in range(LINE)])
+        project.append(np.stack(split(np.kron((basis.T @ basis)[np.ix_(order, order)], np.eye(4)))))
     back = np.zeros((BLOCK, 8, 48))
     for j in range(OWN):
         back[:, j, j * KEEP:(j + 1) * KEEP] = basis.T
     back_h, back_l = split(back.reshape(512, 48))
     back = np.concatenate([back_h, back_h, back_l], axis=1)
-    spread = np.zeros((2, 2, 64, 2, 512))
+    spread = np.zeros((2, 2, 64, 512))
     for r in range(2):
-        spread[r, r, :, 0] = across
-        spread[r, :, :, 1] = 0.5 * across
-    spread_h, spread_l = split(spread.reshape(2, 128, 1024))
+        spread[r, r] = across
+    spread_h, spread_l = split(spread.reshape(2, 128, 512))
     spread = np.concatenate([spread_h, spread_h, spread_l], axis=1)
     return (
         sort.astype(ml_dtypes.bfloat16),
@@ -88,7 +95,7 @@
         squeeze.astype(ml_dtypes.bfloat16),
         twice,
         expand,
-        np.stack(split(project)),
+        np.stack(project),
         back,
         spread,
     )
@@ -106,34 +113,49 @@
 def kernel(
     act_hbm, head_hbm, mom_hbm, sort_hbm, pick_hbm, squeeze_hbm, twice_hbm, expand_hbm, project_hbm, back_hbm, spread_hbm,
     new_out, upd_out,
-    act, mom, sort, pick, squeeze, twice, expand, project, back, spread, stack, windows,
+    act, head, mom, sort, pick, squeeze, twice, expand, project, back, spread, stack, windows,
     a_send, a_recv, tokens, at, gt, grad, grad_row,
     wm_send, wm_recv, pm_send, pm_recv, qm_send, qm_recv, vm, vm_all,
-    coef, vg, vg_all, packed, base_new, base_upd,
+    coef, vg, vg_all, packed, kept, base_new, base_upd,
     load, sa, ra, sz, rz, sg, rg, sgr, rgr, swm, rwm,
     spm, rpm, sqm, rqm, svm, rvm, sqg, rqg, sfg, rfg,
 ):
     core = lax.axis_index("dp")
     t = lax.axis_index("tensor")
-    z, me = lax.div(t, 16), lax.rem(t, 16)
-    y, x = lax.div(me, 4), lax.rem(me, 4)
-
-    def shift(v, by):
-        return lax.rem(v + by % 4, 4)
+    zp, yp, x = lax.div(t, 16), lax.rem(lax.div(t, 4), 4), lax.rem(t, 4)
+    z, y = zp + core * (yp - zp), yp + core * (zp - yp)
+    me = y * 4 + x
+
+    def around(v):
+        return [v] + [lax.rem(v + by, 4) for by in range(1, 4)]
+
+    zs, ys, xs, zps, yps = around(z), around(y), around(x), around(zp), around(yp)
+    z_steps = [v * (16 - 12 * core) for v in zs]
+    y_steps = [v * (4 + 12 * core) for v in ys]
+    y_slots = [v * 4 for v in ys]
+    zp_steps, yp_steps = [v * 16 for v in zps], [v * 4 for v in yps]
 
     def inplane(d):
-        return shift(y, d // 4) * 4 + shift(x, d % 4)
+        return y_slots[d // 4] + xs[d % 4]
+
+    def place(dz, d):
+        return z_steps[dz % 4] + y_steps[d // 4] + xs[d % 4]
 
     def hops(dz, d):
         return sum(min(v, 4 - v) for v in (dz, d // 4, d % 4))
 
     far_first = sorted(range(1, 16), key=lambda d: -hops(0, d))
 
-    def copy(src, dst, ssem, rsem, c, zz, ii):
+    def copy_to(src, dst, ssem, rsem, where):
         return pltpu.make_async_remote_copy(
-            src_ref=src, dst_ref=dst, send_sem=ssem, recv_sem=rsem,
-            device_id=(c, zz * 16 + ii), device_id_type=MESH,
+            src_ref=src, dst_ref=dst, send_sem=ssem, recv_sem=rsem, device_id=where, device_id_type=MESH,
         )
+
+    def copy(src, dst, ssem, rsem, dz, d):
+        return copy_to(src, dst, ssem, rsem, (core, place(dz, d)))
+
+    def copy_across(src, dst, ssem, rsem):
+        return copy_to(src, dst, ssem, rsem, (1 - core, t))
 
     sent = []
     arrived = set()
@@ -148,20 +170,19 @@
         arrived.add(id(c))
 
     barrier = pltpu.get_barrier_semaphore()
-    partners = [(core, z, inplane(d)) for d in far_first]
-    partners += [(core, shift(z, d), me) for d in (2, 1, 3)] + [(1 - core, z, me)]
-    for c, zz, ii in partners:
-        pl.semaphore_signal(barrier, inc=1, device_id=(c, zz * 16 + ii), device_id_type=MESH)
+    partners = [(core, place(0, d)) for d in far_first]
+    partners += [(core, place(d, 0)) for d in (2, 1, 3)] + [(1 - core, t)]
+    for where in partners:
+        pl.semaphore_signal(barrier, inc=1, device_id=where, device_id_type=MESH)
 
     loads = {}
     for k, (name, src, dst) in enumerate((
-        ("act", act_hbm, act), ("sort", sort_hbm, sort), ("squeeze", squeeze_hbm, squeeze), ("head", head_hbm, gt.at[me]),
+        ("act", act_hbm, act), ("sort", sort_hbm.at[core], sort), ("squeeze", squeeze_hbm, squeeze), ("head", head_hbm, head),
         ("mom", mom_hbm, mom), ("pick", pick_hbm, pick), ("twice", twice_hbm, twice), ("expand", expand_hbm, expand),
-        ("project", project_hbm, project), ("back", back_hbm, back), ("spread", spread_hbm.at[core], spread),
+        ("project", project_hbm.at[core], project), ("back", back_hbm, back), ("spread", spread_hbm, spread),
     )):
         loads[name] = pltpu.make_async_copy(src, dst, load.at[k])
         loads[name].start()
-
     loads["act"].wait()
     loads["sort"].wait()
     for tile in range(20):
@@ -206,39 +227,47 @@
             a_send[2 * m + odd, :, 640:768] = both[m * 32:m * 32 + 16]
             a_send[2 * m + odd, :, 768:896] = both[m * 32 + 16:m * 32 + 32]
 
+    def chunk(line, q):
+        return pl.ds(pl.multiple_of((line * 4 + q + core * (q * 4 + line - line * 4 - q)) * 128, 128), 128)
+
     for name in ("mom", "twice"):
         loads[name].wait()
     wm_send[...] = jnp.zeros_like(wm_send)
     coef[core] = jnp.zeros((56, 128), F32)
     for zz in range(LINE):
-        piece = mom[:, zz * ZCOLS:(zz + 1) * ZCOLS]
+        piece = jnp.concatenate([mom[:, chunk(zz, q)] for q in range(4)], axis=1)
         wm_send[zz, :, 0:RBLOCKS] = dot(twice[0, 0:64], piece, NT) + dot(twice[1, 0:64], piece, NT)
+    loads["head"].wait()
+    for tile in range(16):
+        line, row = tile // 4, tile % 4
+        lanes = pl.ds(pl.multiple_of((tile + core * (row * 4 + line - tile)) * 128, 128), 128)
+        gt[me, :, tile * 128:(tile + 1) * 128] = head[:, lanes]
+
     pl.semaphore_wait(barrier, len(partners))
 
     wm_copies = []
 
     def wm_start():
         for d in range(1, 4):
-            to = shift(z, d)
-            wm_copies.append(go(copy(wm_send.at[to], wm_recv.at[z], swm.at[d - 1], rwm.at[d - 1], core, to, me)))
+            to = zs[d]
+            wm_copies.append(go(copy(wm_send.at[to], wm_recv.at[z], swm.at[d - 1], rwm.at[d - 1], d, 0)))
         wm_recv[z] = wm_send[z]
 
     wm_start()
 
 
-    loads["head"].wait()
+    def offset(half, da, db):
+        return (db % 4 * 4 + da % 4) if half == 0 else (da % 4 * 4 + db % 4)
 
     def near2(half, da, db):
-        if half == 0:
-            return shift(y, db) * 4 + shift(x, da)
-        return shift(y, da) * 4 + shift(x, db)
+        return inplane(offset(half, da, db))
 
     g_copies = {}
 
     def g_go(half, slot, rows, sem, to):
-        lanes = pl.ds(half * 1024, 1024)
+        lanes = pl.ds(0, SHARE) if half == 0 else pl.ds(SHARE, TOKENS - SHARE)
         where = gt.at[slot, pl.ds(rows[0], rows[1]), lanes]
-        g_copies[half, sem] = go(copy(where, where, sg.at[half, sem], rg.at[half, sem], core, z, to))
+        g_copies[half, sem] = go(copy(where, where, sg.at[half, sem], rg.at[half, sem], 0, to))
 
     def g_wait(half, sem):
         wait(g_copies[half, sem])
@@ -249,17 +278,17 @@
     def start_a(offsets):
         for d in offsets:
             to = inplane(d)
-            a_copies[d] = go(copy(a_send.at[to], a_recv.at[me], sa.at[d - 1], ra.at[d - 1], core, z, to))
+            a_copies[d] = go(copy(a_send.at[to], a_recv.at[me], sa.at[d - 1], ra.at[d - 1], 0, d))
 
     def start_g1():
         for half in range(2):
-            g_go(half, me, whole, 0, near2(half, 1, 0))
-            g_go(half, me, whole, 1, near2(half, -1, 0))
+            g_go(half, me, whole, 0, offset(half, 1, 0))
+            g_go(half, me, whole, 1, offset(half, -1, 0))
 
     def start_g2():
         for half in range(2):
-            g_go(half, me, whole, 4, near2(half, 0, 1))
-            g_go(half, me, whole, 5, near2(half, 0, -1))
+            g_go(half, me, whole, 4, offset(half, 0, 1))
+            g_go(half, me, whole, 5, offset(half, 0, -1))
 
 
     a_recv[me] = a_send[me]
@@ -271,12 +300,12 @@
         loads[name].wait()
 
     z_copies = {}
-    zu, zd, zo = shift(z, 1), shift(z, -1), shift(z, 2)
+    zu, zd, zo = zs[1], zs[3], zs[2]
     every, first, second = (0, 400), (0, 208), (208, 192)
 
     def z_go(slot, dy, rows, sem, to):
-        where = at.at[slot, shift(y, dy), pl.ds(rows[0], rows[1]), :]
-        z_copies[dy, sem] = go(copy(where, where, sz.at[dy, sem], rz.at[dy, sem], core, to, me))
+        where = at.at[slot, ys[dy], pl.ds(rows[0], rows[1]), :]
+        z_copies[dy, sem] = go(copy(where, where, sz.at[dy, sem], rz.at[dy, sem], to, 0))
 
     def z_wait(dy, sem):
         wait(z_copies[dy, sem])
@@ -286,7 +315,7 @@
             d = (-dy % 4) * 4 + (-dx % 4)
             if d:
                 wait(a_copies[d])
-        line = shift(y, dy)
+        line = ys[dy]
         for src in range(4):
             here = a_recv.at[line * 4 + src]
             top, low = slice(src * 32, src * 32 + 16), slice(src * 32 + 16, src * 32 + 32)
@@ -297,21 +326,21 @@
             tokens[top, 512:640] = here[:, 640:768]
             tokens[low, 512:640] = here[:, 768:896]
         at[z, line] = dot(pick[...], tokens[...], NT).astype(BF16)
-        z_go(z, dy, every, 0, zu)
-        z_go(z, dy, every, 1, zd)
+        z_go(z, dy, every, 0, 1)
+        z_go(z, dy, every, 1, 3)
 
     def z_relay(dy):
         z_wait(dy, 0)
-        z_go(zd, dy, first, 2, zu)
+        z_go(zd, dy, first, 2, 1)
         z_wait(dy, 1)
-        z_go(zu, dy, second, 3, zd)
+        z_go(zu, dy, second, 3, 3)
 
     def g_relay(j, da):
         for half in range(2):
             g_wait(half, 4 + 4 * j)
-            g_go(half, near2(half, da, -1), upper, 6 + 4 * j, near2(half, 0, 1))
+            g_go(half, near2(half, da, -1), upper, 6 + 4 * j, offset(half, 0, 1))
             g_wait(half, 5 + 4 * j)
-            g_go(half, near2(half, da, 1), lower, 7 + 4 * j, near2(half, 0, -1))
+            g_go(half, near2(half, da, 1), lower, 7 + 4 * j, offset(half, 0, -1))
 
     def regroup_w(src, dst):
         for q in range(PLANE):
@@ -327,15 +356,15 @@
         out = []
         for d in far_first:
             to = inplane(d)
-            out.append(go(copy(src.at[to], dst.at[me], ssem.at[d - 1], rsem.at[d - 1], core, z, to)))
+            out.append(go(copy(src.at[to], dst.at[me], ssem.at[d - 1], rsem.at[d - 1], 0, d)))
         dst[me] = src[me]
         return out
 
     def line_start(src, dst, ssem, rsem):
-        out = {0: go(copy(src.at[z], dst.at[core, z], ssem.at[1, 0], rsem.at[1, 0], 1 - core, z, me))}
+        out = {0: go(copy_across(src.at[z], dst.at[core, z], ssem.at[1, 0], rsem.at[1, 0]))}
         for d in (2, 1, 3):
-            to = shift(z, d)
-            out[d] = go(copy(src.at[to], dst.at[core, z], ssem.at[0, d], rsem.at[0, d], core, to, me))
+            to = zs[d]
+            out[d] = go(copy(src.at[to], dst.at[core, z], ssem.at[0, d], rsem.at[0, d], d, 0))
         dst[core, z] = src[z]
         return out
 
@@ -343,8 +372,8 @@
         forward = [out[0]]
         for d in (1, 3, 2):
             wait(out[d])
-            where = dst.at[core, shift(z, -d)]
-            forward.append(go(copy(where, where, ssem.at[1, d], rsem.at[1, d], 1 - core, z, me)))
+            where = dst.at[core, zs[-d % 4]]
+            forward.append(go(copy_across(where, where, ssem.at[1, d], rsem.at[1, d])))
         return forward
 
     def apply_project(w):
@@ -352,6 +381,13 @@
         return dot(project[0], high, NN) + dot(project[0], low, NN) + dot(project[1], high, NN)
 
     pm_copies, qm_copies, vm_copies = [], [], []
+
+    def mean_kept(zz, q):
+        return kept[0, zz, :, q * 128:(q + 1) * 128] + kept[1, q, :, zz * 128:(zz + 1) * 128]
+
+    def own_part(ref, zz, q):
+        lanes = pl.ds(pl.multiple_of((q + core * (zz - q)) * 128, 128), 128)
+        return ref[zz + core * (q - zz), :, lanes]
 
     def momentum_step(which):
         if which == 1:
@@ -372,33 +408,33 @@
         else:
             for c in line_end(vm_copies[0], vm_all, svm, rvm):
                 wait(c)
+            for r in range(2):
+                for zz in range(LINE):
+                    high, low = parts(vm_all[r, zz])
+                    kept[r, zz] = dot(jnp.concatenate([high, low, high], axis=0), expand[...], TN)[0:RBLOCKS]
             for zz in range(LINE):
-                cols = slice(zz * ZCOLS, (zz + 1) * ZCOLS)
-                pair = []
-                for r in range(2):
-                    high, low = parts(vm_all[r, zz])
-                    pair.append(dot(jnp.concatenate([high, low, high], axis=0), expand[...], TN)[0:RBLOCKS])
-                base_upd[:, cols] = F32(0.45) * (pair[0] + pair[1])
-                own = jnp.where(core == 0, pair[0], pair[1])
-                base_new[:, cols] = F32(0.9) * (mom[:, cols].astype(F32) - own)
+                for q in range(4):
+                    cols = slice(zz * ZCOLS + q * 128, zz * ZCOLS + (q + 1) * 128)
+                    base_upd[:, cols] = F32(0.45) * mean_kept(zz, q)
+                    base_new[:, cols] = F32(0.9) * (mom[:, cols].astype(F32) - own_part(kept.at[core], zz, q))
 
     def near_chunks():
         for half in range(2):
             g_wait(half, 0)
-            g_go(half, near2(half, -1, 0), upper, 2, near2(half, 1, 0))
+            g_go(half, near2(half, -1, 0), upper, 2, offset(half, 1, 0))
             g_wait(half, 1)
-            g_go(half, near2(half, 1, 0), lower, 3, near2(half, -1, 0))
+            g_go(half, near2(half, 1, 0), lower, 3, offset(half, -1, 0))
         for half in range(2):
             for j, da in ((1, -1), (2, 1)):
-                g_go(half, near2(half, da, 0), whole, 4 + 4 * j, near2(half, 0, 1))
-                g_go(half, near2(half, da, 0), whole, 5 + 4 * j, near2(half, 0, -1))
+                g_go(half, near2(half, da, 0), whole, 4 + 4 * j, offset(half, 0, 1))
+                g_go(half, near2(half, da, 0), whole, 5 + 4 * j, offset(half, 0, -1))
 
     def far_chunk():
         for half in range(2):
             g_wait(half, 2)
             g_wait(half, 3)
-            g_go(half, near2(half, 2, 0), whole, 16, near2(half, 0, 1))
-            g_go(half, near2(half, 2, 0), whole, 17, near2(half, 0, -1))
+            g_go(half, near2(half, 2, 0), whole, 16, offset(half, 0, 1))
+            g_go(half, near2(half, 2, 0), whole, 17, offset(half, 0, -1))
 
     for step in ORDER:
         kind, which = step[0], step[1:]
@@ -435,15 +471,15 @@
     grad[...] = rows.reshape(LINE, RBLOCKS, ZCOLS)
     square = jnp.sum(jnp.sum(rows * rows, axis=0, keepdims=True), axis=1, keepdims=True)
     for d in range(1, 4):
-        to = shift(z, d)
-        grad_copies.append(go(copy(grad.at[to], grad_row.at[z], sgr.at[d - 1], rgr.at[d - 1], core, to, me)))
+        to = zs[d]
+        grad_copies.append(go(copy(grad.at[to], grad_row.at[z], sgr.at[d - 1], rgr.at[d - 1], d, 0)))
     grad_row[z] = grad[z]
     mine = lax.broadcasted_iota(jnp.int32, (40, 128), 1) // 64 == core
     high, low = parts(acc[320:360] + acc[360:400])
     own = dot(high, twice[0], NT) + dot(low, twice[0], NT) + dot(high, twice[1], NT)
     coef[core, 0:40, :] = jnp.where(mine, own, F32(0.0))
     coef[core, 48:56, :] = jnp.where(mine[0:8], jnp.broadcast_to(square, (8, 128)), F32(0.0))
-    share = go(copy(coef.at[core], coef.at[core], sfg.at[0], rfg.at[0], 1 - core, z, me))
+    share = go(copy_across(coef.at[core], coef.at[core], sfg.at[0], rfg.at[0]))
     v_copies = {}
     wait(share)
     high, low = parts(coef[0, 0:48] + coef[1, 0:48])
@@ -453,9 +489,9 @@
     vg[...] = result.reshape(64, 8, 128) + jnp.where(row == 5, sums, F32(0.0))[None]
     for dz, d in sorted(((dz, d) for dz in range(4) for d in range(16)), key=lambda v: -hops(*v)):
         if dz or d:
-            zz, ii = shift(z, dz), inplane(d)
-            v_copies[dz, d] = go(copy(
-                vg.at[zz * 16 + ii], vg_all.at[t], sqg.at[dz, d], rqg.at[dz, d], core, zz, ii))
+            to = zp_steps[dz] + yp_steps[d // 4] + xs[d % 4]
+            v_copies[dz, d] = go(copy_to(
+                vg.at[to], vg_all.at[t], sqg.at[dz, d], rqg.at[dz, d], (core, to)))
     vg_all[t] = vg[t]
     for step in MSTEPS:
         momentum_step(step)
@@ -465,18 +501,26 @@
     square = jnp.sum(vg_all[:, 5:6, :], axis=0)
     factors = jnp.minimum(F32(1.0), 1.0 / jnp.sqrt(square / (RBLOCKS * BLOCK * COLS) + 1e-06))
     factor = jnp.where(core == 0, factors[:, 0:1], factors[:, 127:128])
+    for src in range(64):
+        zz, yy, xx = src // 16, src // 4 % 4, src % 4
+        for r, line, i in ((0, zz, yy * 4 + xx), (1, yy, zz * 4 + xx)):
+            top = line * RBLOCKS + OWN * i
+            packed[r, top:top + OWN, :] = vg_all[src, 0:OWN, :]
+    for r in range(2):
+        high, low = parts(packed[r] * factors)
+        result = dot(jnp.concatenate([high, low, high], axis=1), spread[r], NN)
+        kept[r] = result.reshape(LINE, RBLOCKS, ZCOLS)
     for zz in range(LINE):
-        for i in range(PLANE):
-            packed[zz * RBLOCKS + OWN * i:zz * RBLOCKS + OWN * (i + 1), :] = vg_all[zz * 16 + i, 0:OWN, :]
-    high, low = parts(packed[...] * factors)
-    kept = dot(jnp.concatenate([high, low, high], axis=1), spread[...], NN)
+        for q in range(4):
+            cols = slice(zz * ZCOLS + q * 128, zz * ZCOLS + (q + 1) * 128)
+            upd_out[:, cols] = (base_upd[:, cols] + F32(0.5) * mean_kept(zz, q)).astype(BF16)
     for c in grad_copies:
         wait(c)
     for zz in range(LINE):
-        cols = slice(zz * ZCOLS, (zz + 1) * ZCOLS)
-        rows = slice(zz * RBLOCKS, (zz + 1) * RBLOCKS)
-        new_out[:, cols] = (base_new[:, cols] + (factor * grad_row[zz] - kept[rows, 0:512])).astype(BF16)
-        upd_out[:, cols] = (base_upd[:, cols] + kept[rows, 512:1024]).astype(BF16)
+        for q in range(4):
+            cols = slice(zz * ZCOLS + q * 128, zz * ZCOLS + (q + 1) * 128)
+            more = factor * own_part(grad_row, zz, q) - own_part(kept.at[core], zz, q)
+            new_out[:, cols] = (base_new[:, cols] + more).astype(BF16)
     for c in sent:
         if id(c) not in arrived:
             c.wait_recv()
@@ -490,8 +534,9 @@
     hbm = pl.BlockSpec(memory_space=pltpu.HBM)
     scratch = [
         pltpu.VMEM((32, RBLOCKS * BLOCK), BF16),
+        pltpu.VMEM((32, TOKENS), BF16),
         pltpu.VMEM((RBLOCKS, COLS), BF16),
-    ] + [pltpu.VMEM(c.shape, BF16) for c in consts[:-1]] + [pltpu.VMEM(consts[-1].shape[1:], BF16)] + [
+    ] + [pltpu.VMEM(c.shape[1:] if k in (0, 5) else c.shape, BF16) for k, c in enumerate(consts)] + [
         pltpu.VMEM((640, 256), BF16),
         pltpu.VMEM((2, 256, 384), BF16),
         pltpu.VMEM((PLANE, 16, 896), BF16),
@@ -512,7 +557,8 @@
         pltpu.VMEM((2, 56, 128), F32),
         pltpu.VMEM((64, 8, 128), F32),
         pltpu.VMEM((64, 8, 128), F32),
-        pltpu.VMEM((LINE * RBLOCKS, 128), F32),
+        pltpu.VMEM((2, LINE * RBLOCKS, 128), F32),
+        pltpu.VMEM((2, LINE, RBLOCKS, ZCOLS), F32),
         pltpu.VMEM((RBLOCKS, COLS), F32),
         pltpu.VMEM((RBLOCKS, COLS), F32),
         dma((11,)),

time: 47.2 us -> 46.3 us (0.981)
  Pallas kernels: 46.3 us -> 45.4 us
    pallas_call x1, Pallas kernels: 45.4 us -> 44.6 us  [body(): pl.pallas_call(kernel, out_shape=(pltpu.VMEM((RBLOCKS, COLS), BF16), pltp...]
where the time goes in v4:
time: 46.3 us; the launch traced here: 46.1 us
  Pallas kernels  45.4 us (98%)
  between operations  0.64 us (1%)
    pallas_call x1, Pallas kernels, body(): pl.pallas_call(kernel, out_shape=(pltpu.VMEM((RBLOCKS, COLS), BF16), pltp...  44.6 us

profile of v4, /device:TPU:1, one launch (start us, length us, event | category | flops | bytes accessed | tf_op | source)
XLA Modules:
  0.0 46.1 jit_solution(12999706667601803756)
XLA Ops:
  0.6 44.6 %shard_map.122 = (bf16[80,2048]{1,0:T(8,128)(2,1)S(1)}, bf16[80,2048]{1,0:T(8,128)(2,1)S(1)}) custom-call(bf16[32,5120]{1,0:T(8,128)(2,1)} %act_hbm.1, bf16[32,2048]{1,0:T(8,128)(2,1)} %bitcast.5, bf16[80,2048]{1,0:T(8,128)(2,1)} %bitcast.4, bf16[2,256,256]{2,1,0:T(8,128)(2,1)} %constant.16.clone.sort_hbm, bf16[400,640]{1,0:T(8,128)(2,1)} %constant.17.clone.pick_hbm, ...), custom_call_target="tpu_custom_call" | custom-call | tf_op jit(solution)/shard_map/pallas_call | solution.py:568
  45.2 0.9 %shard_map.123 = (bf16[80,2048]{1,0:T(8,128)(2,1)}, bf16[80,2048]{1,0:T(8,128)(2,1)}) custom-call(bf16[80,2048]{1,0:T(8,128)(2,1)S(1)} %get-tuple-element.6.new_ref, bf16[80,2048]{1,0:T(8,128)(2,1)S(1)} %get-tuple-element.7.upd_ref), custom_call_target="tpu_custom_call" | custom-call | tf_op jit(solution)/shard_map/pallas_call | solution.py:593

commit v5 on v4

--- a/solution.py
+++ b/solution.py
@@ -27,7 +27,7 @@
 NT = (((1,), (1,)), ((), ()))
 TN = (((0,), (0,)), ((), ()))
 NN = (((1,), (0,)), ((), ()))
-ORDER = ("a0", "s", "a1", "a3", "a2", "m1", "f", "g0", "z0", "g1", "g2", "z1", "m2", "g3", "z3", "z2", "m3")
+ORDER = ("a0", "s", "a1", "a3", "a2", "m1", "f", "z0", "g0", "g1", "g2", "z1", "m2", "g3", "z3", "z2", "m3")
 START = "1A2"
 MSTEPS = (4,)
 AORD = (1, 3, 2, 4, 12, 5, 7, 13, 15, 6, 14, 8, 9, 11, 10)
@@ -227,6 +227,55 @@
             a_send[2 * m + odd, :, 640:768] = both[m * 32:m * 32 + 16]
             a_send[2 * m + odd, :, 768:896] = both[m * 32 + 16:m * 32 + 32]
 
+    loads["head"].wait()
+    for tile in range(16):
+        line, row = tile // 4, tile % 4
+        lanes = pl.ds(pl.multiple_of((tile + core * (row * 4 + line - tile)) * 128, 128), 128)
+        gt[me, :, tile * 128:(tile + 1) * 128] = head[:, lanes]
+
+    pl.semaphore_wait(barrier, len(partners))
+
+
+    def offset(half, da, db):
+        return (db % 4 * 4 + da % 4) if half == 0 else (da % 4 * 4 + db % 4)
+
+    def near2(half, da, db):
+        return inplane(offset(half, da, db))
+
+    g_copies = {}
+
+    def g_go(half, slot, rows, sem, to):
+        lanes = pl.ds(0, SHARE) if half == 0 else pl.ds(SHARE, TOKENS - SHARE)
+        where = gt.at[slot, pl.ds(rows[0], rows[1]), lanes]
+        g_copies[half, sem] = go(copy(where, where, sg.at[half, sem], rg.at[half, sem], 0, to))
+
+    def g_wait(half, sem):
+        wait(g_copies[half, sem])
+
+    whole, upper, lower = (0, 32), (0, 16), (16, 16)
+
+    a_copies = {}
+    def start_a(offsets):
+        for d in offsets:
+            to = inplane(d)
+            a_copies[d] = go(copy(a_send.at[to], a_recv.at[me], sa.at[d - 1], ra.at[d - 1], 0, d))
+
+    def start_g1():
+        for half in range(2):
+            g_go(half, me, whole, 0, offset(half, 1, 0))
+            g_go(half, me, whole, 1, offset(half, -1, 0))
+
+    def start_g2():
+        for half in range(2):
+            g_go(half, me, whole, 4, offset(half, 0, 1))
+            g_go(half, me, whole, 5, offset(half, 0, -1))
+
+
+    a_recv[me] = a_send[me]
+    tokens[...] = jnp.zeros_like(tokens)
+    for step in START:
+        {"A": lambda: start_a(AORD), "1": start_g1, "2": start_g2}[step]()
+
     def chunk(line, q):
         return pl.ds(pl.multiple_of((line * 4 + q + core * (q * 4 + line - line * 4 - q)) * 128, 128), 128)
 
@@ -237,14 +286,6 @@
     for zz in range(LINE):
         piece = jnp.concatenate([mom[:, chunk(zz, q)] for q in range(4)], axis=1)
         wm_send[zz, :, 0:RBLOCKS] = dot(twice[0, 0:64], piece, NT) + dot(twice[1, 0:64], piece, NT)
-    loads["head"].wait()
-    for tile in range(16):
-        line, row = tile // 4, tile % 4
-        lanes = pl.ds(pl.multiple_of((tile + core * (row * 4 + line - tile)) * 128, 128), 128)
-        gt[me, :, tile * 128:(tile + 1) * 128] = head[:, lanes]
-
-    pl.semaphore_wait(barrier, len(partners))
-
     wm_copies = []
 
     def wm_start():
@@ -254,47 +295,6 @@
         wm_recv[z] = wm_send[z]
 
     wm_start()
-
-
-    def offset(half, da, db):
-        return (db % 4 * 4 + da % 4) if half == 0 else (da % 4 * 4 + db % 4)
-
-    def near2(half, da, db):
-        return inplane(offset(half, da, db))
-
-    g_copies = {}
-
-    def g_go(half, slot, rows, sem, to):
-        lanes = pl.ds(0, SHARE) if half == 0 else pl.ds(SHARE, TOKENS - SHARE)
-        where = gt.at[slot, pl.ds(rows[0], rows[1]), lanes]
-        g_copies[half, sem] = go(copy(where, where, sg.at[half, sem], rg.at[half, sem], 0, to))
-
-    def g_wait(half, sem):
-        wait(g_copies[half, sem])
-
-    whole, upper, lower = (0, 32), (0, 16), (16, 16)
-
-    a_copies = {}
-    def start_a(offsets):
-        for d in offsets:
-            to = inplane(d)
-            a_copies[d] = go(copy(a_send.at[to], a_recv.at[me], sa.at[d - 1], ra.at[d - 1], 0, d))
-
-    def start_g1():
-        for half in range(2):
-            g_go(half, me, whole, 0, offset(half, 1, 0))
-            g_go(half, me, whole, 1, offset(half, -1, 0))
-
-    def start_g2():
-        for half in range(2):
-            g_go(half, me, whole, 4, offset(half, 0, 1))
-            g_go(half, me, whole, 5, offset(half, 0, -1))
-
-
-    a_recv[me] = a_send[me]
-    tokens[...] = jnp.zeros_like(tokens)
-    for step in START:
-        {"A": lambda: start_a(AORD), "1": start_g1, "2": start_g2}[step]()
 
     for name in ("pick", "expand", "project", "back", "spread"):
         loads[name].wait()
@@ -514,13 +514,13 @@
         for q in range(4):
             cols = slice(zz * ZCOLS + q * 128, zz * ZCOLS + (q + 1) * 128)
             upd_out[:, cols] = (base_upd[:, cols] + F32(0.5) * mean_kept(zz, q)).astype(BF16)
+            base_new[:, cols] = base_new[:, cols] - own_part(kept.at[core], zz, q)
     for c in grad_copies:
         wait(c)
     for zz in range(LINE):
         for q in range(4):
             cols = slice(zz * ZCOLS + q * 128, zz * ZCOLS + (q + 1) * 128)
-            more = factor * own_part(grad_row, zz, q) - own_part(kept.at[core], zz, q)
-            new_out[:, cols] = (base_new[:, cols] + more).astype(BF16)
+            new_out[:, cols] = (base_new[:, cols] + factor * own_part(grad_row, zz, q)).astype(BF16)
     for c in sent:
         if id(c) not in arrived:
             c.wait_recv()

time: 46.3 us -> 46.3 us (level)
  no operation moved by 1% of the time
where the time goes in v5:
time: 46.3 us; the launch traced here: 46.1 us
  Pallas kernels  45.5 us (98%)
  between operations  0.64 us (1%)
    pallas_call x1, Pallas kernels, body(): pl.pallas_call(kernel, out_shape=(pltpu.VMEM((RBLOCKS, COLS), BF16), pltp...  44.6 us

profile of v5, /device:TPU:1, one launch (start us, length us, event | category | flops | bytes accessed | tf_op | source)
XLA Modules:
  0.0 46.1 jit_solution(16500670658167261808)
XLA Ops:
  0.6 44.6 %shard_map.122 = (bf16[80,2048]{1,0:T(8,128)(2,1)S(1)}, bf16[80,2048]{1,0:T(8,128)(2,1)S(1)}) custom-call(bf16[32,5120]{1,0:T(8,128)(2,1)} %act_hbm.1, bf16[32,2048]{1,0:T(8,128)(2,1)} %bitcast.5, bf16[80,2048]{1,0:T(8,128)(2,1)} %bitcast.4, bf16[2,256,256]{2,1,0:T(8,128)(2,1)} %constant.16.clone.sort_hbm, bf16[400,640]{1,0:T(8,128)(2,1)} %constant.17.clone.pick_hbm, ...), custom_call_target="tpu_custom_call" | custom-call | tf_op jit(solution)/shard_map/pallas_call | solution.py:568
  45.2 0.9 %shard_map.123 = (bf16[80,2048]{1,0:T(8,128)(2,1)}, bf16[80,2048]{1,0:T(8,128)(2,1)}) custom-call(bf16[80,2048]{1,0:T(8,128)(2,1)S(1)} %get-tuple-element.6.new_ref, bf16[80,2048]{1,0:T(8,128)(2,1)S(1)} %get-tuple-element.7.upd_ref), custom_call_target="tpu_custom_call" | custom-call | tf_op jit(solution)/shard_map/pallas_call | solution.py:593
